TPU v7x, 512 devices: a whole 4x8x8 slice. The times are simulated.
512 devices in a mesh: row: 32 (over y, x), col: 16 (over z, core).
Axes of the slice: x: 4, y: 8, z: 8, core: 2. Of those that a mesh axis runs over, the one named last changes fastest.
Arguments:
- a_vals: bfloat16 [32, 256, 64, 2048], P('row', 'col'), may hold values from -0.25 to 0.25
- a_cols: int32 [32, 256, 32], P('row', 'col'), may hold values from 0 to 767, as said below
- a_count: int32 [32, 256], P('row', 'col'), may hold values from 4 to 32, as said below
- p_vals: bfloat16 [32, 256, 64, 128], P('row', 'col'), may hold values from -6 to 6
- p_cols: int32 [32, 256, 2], P('row', 'col'), may hold values from 0 to 15, as said below
- r_vals: bfloat16 [32, 256, 64, 128], P('row', 'col'), may hold values from -0.125 to 0.125
- r_cols: int32 [32, 256, 2], P('row', 'col'), may hold values from 0 to 15, as said below
Outputs:
- coarse: float32 [32, 1024, 960], P('row', 'col')
Inputs may be any that keep to these rules, and one draw needn't show every extreme that they name: `a_cols`: the entries of a row are distinct. Every entry is s * 256 + t with t = (q + o) mod 256 for the row's block q and some o with -8 <= o <= 8; q itself appears with s = 0, 1 and 2, and every row has an entry with o = 8 or o = -8. `a_count`: in each plane, the 31 blocks nearest one block (around the plane) have 32 live slots; the other rows have from 4 to min(10, 32). `p_cols`: A row of block q holds, in either order, the aggregate q // 16 and the aggregate beside it on the side of q's half of its aggregate: (q // 16 - 1) mod 16 where q % 16 < 8, else (q // 16 + 1) mod 16. `r_cols`: A row of block q holds the same two aggregates as p_cols[z, q], in an order of its own.
All inputs are finite; a program needn't handle non-finite values.
Results may differ from a plain program's by a relative error of at most 0.0029.
Values may be sent and summed in bfloat16 or wider, within the bound.
No kernel may reach another device: no remote copies, remote signals or barrier semaphores. Data moves between devices by JAX's collectives and lax.ppermute only.
A program may use at most 128 MiB of HBM per device.

v0:
```python
import math

import jax
import jax.numpy as jnp
from jax import lax
from jax.sharding import PartitionSpec as P

PLANE = 256
AGG = 16
WIN = 8
NCP = 16


def with_halo(cells, sides, width, closed):
    for axis, dim in sides:
        count = lax.axis_size(axis)
        ends = count if closed else count - 1
        head = lax.slice_in_dim(cells, 0, width, axis=dim)
        tail = lax.slice_in_dim(cells, cells.shape[dim] - width, cells.shape[dim], axis=dim)
        cells = jnp.concatenate(
            [
                lax.ppermute(tail, axis, [(i, (i + 1) % count) for i in range(ends)]),
                cells,
                lax.ppermute(head, axis, [((i + 1) % count, i) for i in range(ends)]),
            ],
            axis=dim,
        )
    return cells


def shifted(value, axis, steps):
    count = lax.axis_size(axis)
    pairs = [(source, (source + steps) % count) for source in range(count)]
    return lax.ppermute(value, axis, pairs)


def frames(values, columns, first_block):
    planes_dev, section_rows, block_size, _ = values.shape
    blocks = first_block + jnp.arange(section_rows, dtype=jnp.int32)
    own_agg = blocks // AGG
    slot_window = (columns - own_agg[None, :, None] + 1) % NCP
    onehot = (slot_window[..., None] == jnp.arange(4, dtype=jnp.int32)).astype(jnp.bfloat16)
    spread = values.reshape((planes_dev, section_rows, block_size, columns.shape[2], block_size))
    framed = jnp.einsum("zqbmc,zqmj->zqbjc", spread, onehot, preferred_element_type=jnp.float32)
    return framed.astype(jnp.bfloat16).reshape(
        (planes_dev, section_rows, block_size, 4 * block_size)
    )


def body(a_vals, a_cols, a_count, p_vals, p_cols, r_vals, r_cols):
    planes_dev, section_rows, block_size, _ = a_vals.shape
    slot_count = a_cols.shape[2]
    own_aggs = section_rows // AGG
    seg_start = lax.axis_index("col") * section_rows
    framed = frames(p_vals, p_cols, seg_start)
    widened = with_halo(framed, (("col", 1),), WIN, True)
    stacked = with_halo(widened, (("row", 0),), 1, False)
    ext_rows = stacked.shape[1]
    flat_rows = stacked.reshape((-1, block_size, 4 * block_size))
    local_q = jnp.arange(section_rows, dtype=jnp.int32)
    blocks = seg_start + local_q
    band_of = a_cols // PLANE
    target = a_cols % PLANE
    offset_of = (target - blocks[None, :, None] + WIN) % PLANE - WIN
    plane_at = jnp.arange(planes_dev, dtype=jnp.int32)[:, None, None] + band_of
    rows_at = plane_at * ext_rows + local_q[None, :, None] + WIN + offset_of
    agg_shift = (target // AGG - (blocks // AGG)[None, :, None] + 1) % NCP - 1
    three = jnp.arange(3, dtype=jnp.int32)
    four = jnp.arange(4, dtype=jnp.int32)
    live_slot = jnp.arange(slot_count, dtype=jnp.int32)[None, None, :] < a_count[..., None]
    band_hit = band_of[..., None] == three
    frame_hit = three[:, None] == four[None, :] + agg_shift[..., None, None]
    placing = (
        band_hit[..., :, None, None] & frame_hit[..., None, :, :] & live_slot[..., None, None, None]
    ).astype(jnp.float32)
    count_rows = planes_dev * section_rows
    group_rows = math.gcd(4, count_rows)
    turns_rows = count_rows // group_rows
    row_vals = a_vals.reshape((turns_rows, group_rows, block_size, slot_count, block_size))
    row_index = rows_at.reshape((turns_rows, group_rows, slot_count))
    row_place = placing.reshape((turns_rows, group_rows, slot_count, 3, 3, 4))

    def slot_terms(coupling_weight, slot_rows, slot_place):
        selected_entries = jnp.take(flat_rows, slot_rows, axis=0).reshape(
            (slot_rows.shape[0], block_size, 4, block_size)
        )
        triple_product = jnp.einsum(
            "pul,uloc->upoc", coupling_weight, selected_entries, preferred_element_type=jnp.float32
        )
        return jnp.einsum(
            "kbje,ksij->bsie", triple_product, slot_place, precision=lax.Precision.HIGHEST
        )

    def one_row(coupling_weight, slot_rows, slot_place):
        return slot_terms(coupling_weight, slot_rows, slot_place).astype(jnp.bfloat16)

    def row_group(row_items):
        return jax.vmap(one_row)(row_items[0], row_items[1], row_items[2])

    fine_rows = lax.map(row_group, (row_vals, row_index, row_place))
    fine_rows = fine_rows.reshape((planes_dev, section_rows, block_size, 3, 3, block_size))
    restrict = r_vals.reshape((planes_dev, section_rows, block_size, r_cols.shape[2], block_size))
    partial_value = jnp.einsum(
        "zqbld,zqbsie->zqldsie", restrict, fine_rows, preferred_element_type=jnp.float32
    )
    offset = (r_cols - (blocks // AGG)[None, :, None] + 1) % NCP - 1
    local_agg = local_q // AGG + 1
    target_row = local_agg[None, :, None] + offset
    row_hit = target_row[..., None] == jnp.arange(own_aggs + 2, dtype=jnp.int32)
    col_hit = (
        jnp.arange(5, dtype=jnp.int32)[:, None] == three[None, :] - offset[..., None, None] + 1
    )
    placing_r = (row_hit[..., :, None, None] & col_hit[..., None, :, :]).astype(jnp.float32)
    gathered = jnp.einsum(
        "zqldsie,zqluri->zudsre", partial_value, placing_r, precision=lax.Precision.HIGHEST
    )
    gathered = gathered.reshape((planes_dev, own_aggs + 2, block_size, 15 * block_size))
    from_above = shifted(gathered[:, 0], "col", -1)
    from_below = shifted(gathered[:, own_aggs + 1], "col", 1)
    owned = gathered[:, 1 : own_aggs + 1]
    owned = owned.at[:, own_aggs - 1].add(from_above)
    owned = owned.at[:, 0].add(from_below)
    return owned.reshape((planes_dev, own_aggs * block_size, 15 * block_size))


def solution(mesh):
    return jax.shard_map(
        body,
        mesh=mesh,
        in_specs=(
            P("row", "col", None, None),
            P("row", "col", None),
            P("row", "col"),
            P("row", "col", None, None),
            P("row", "col", None),
            P("row", "col", None, None),
            P("row", "col", None),
        ),
        out_specs=P("row", "col", None),
        check_vma=False,
    )
```

profile of v0, /device:TPU:30, one launch (start us, length us, event | category | flops | bytes accessed | tf_op | source)
XLA Modules:
  0.0 330.4 jit_solution(3455467718165998492)
XLA Ops:
  4.1 8.5 %collective-permute-start.1 = (bf16[1,8,64,256]{3,2,1,0:T(8,128)(2,1)S(1)}, bf16[1,8,64,256]{3,2,1,0:T(8,128)(2,1)S(1)}, u32[]{:S(2)}, u32[]{:S(2)}) collective-permute-start(bf16[1,8,64,256]{3,2,1,0:T(8,128)(2,1)S(1)} %get-tuple-element.78), channel_id=1, source_target_pairs={{1,0},{2,1},{3,2},{4,3},{5,4},{6,5},{7,6},{8,7},{9,8},{10,9},{11,1... | collective-permute-start | bytes 786440 | tf_op jit(solution)/shard_map/ppermute | solution.py:24
  14.6 12.9 %reshape.303 = bf16[4,4,64,32,64]{4,3,2,1,0:T(8,128)(2,1)} reshape(bf16[1,16,64,2048]{3,2,1,0:T(8,128)(2,1)} %param.13) | data formatting | bytes 8388608 | tf_op jit(solution)/shard_map/reshape | solution.py:79
  28.7 4.6 %collective-permute-start.2 = (bf16[1,32,64,256]{3,2,1,0:T(8,128)(2,1)S(1)}, bf16[1,32,64,256]{3,2,1,0:T(8,128)(2,1)S(1)}, u32[]{:S(2)}, u32[]{:S(2)}) collective-permute-start(bf16[1,32,64,256]{3,2,1,0:T(8,128)(2,1)S(1)} %constant_dynamic-update-slice_fusion), channel_id=1, source_target_pairs={{0,16},{16,32},{32,48},{48,64},{64,80},{80,96},{96,112},{112,128},... | collective-permute-start | bytes 3145736 | tf_op jit(solution)/shard_map/ppermute | solution.py:22
  36.1 13.8 %collective-permute-done.2 = bf16[1,32,64,256]{3,2,1,0:T(8,128)(2,1)S(1)} collective-permute-done((bf16[1,32,64,256]{3,2,1,0:T(8,128)(2,1)S(1)}, bf16[1,32,64,256]{3,2,1,0:T(8,128)(2,1)S(1)}, u32[]{:S(2)}, u32[]{:S(2)}) %collective-permute-start.2) | collective-permute-done | bytes 1048608 | tf_op jit(solution)/shard_map/ppermute | solution.py:22
  49.9 7.4 %collective-permute-done.3 = bf16[1,32,64,256]{3,2,1,0:T(8,128)(2,1)S(1)} collective-permute-done((bf16[1,32,64,256]{3,2,1,0:T(8,128)(2,1)S(1)}, bf16[1,32,64,256]{3,2,1,0:T(8,128)(2,1)S(1)}, u32[]{:S(2)}, u32[]{:S(2)}) %collective-permute-start.3) | collective-permute-done | bytes 1048608 | tf_op jit(solution)/shard_map/ppermute | solution.py:24
  57.7 227.5 %while.12 = (s32[]{:T(128)}, bf16[4,4,64,3,3,64]{5,4,2,3,1,0:T(4,128)(2,1)}, f32[4,4,32,3,3,4]{2,4,5,3,1,0:T(4,128)S(1)}, bf16[4,4,64,32,64]{4,3,2,1,0:T(8,128)(...) while((s32[]{:T(128)}, bf16[4,4,64,3,3,64]{5,4,2,3,1,0:T(4,128)(2,1)}, ...), condition=%wide.region_1.2_spmd, body=%wide.region_0.1_spmd.sunk | while | flops 497174656 | bytes 58565464 | solution.py:100
  58.0 2.8 gather_fusion
  60.8 12.9 %gather.11 = bf16[4,32,64,4,64]{4,3,2,1,0:T(4,128)(2,1)} reshape(bf16[128,64,256]{2,1,0:T(8,128)(2,1)} %gather_fusion) | data formatting | bytes 8388608 | tf_op jit(solution)/shard_map/while/body/eval_jaxpr/vmap(jit(_take))/gather | solution.py:84
  73.7 6.1 %broadcast_select_fusion.2 = bf16[4,32,64,4,64]{4,3,2,1,0:T(4,128)(2,1)S(1)} fusion(bf16[4,32,64,4,64]{4,3,2,1,0:T(4,128)(2,1)} %gather.11, pred[4,32]{1,0:T(4,128)(4,1)S(1)} %compare_and_fusion.2), kind=kLoop, calls=%fused_computation.5.clone.1 | loop fusion | flops 2097152 | bytes 8388736 | tf_op jit(solution)/shard_map/while/body/eval_jaxpr/vmap(jit(_take))/select_n | solution.py:84
  81.8 7.0 %convolution_bitcast_fusion.2 = f32[4,32,64,4,64,1]{4,2,3,1,0,5:T(8,128)} fusion(bf16[4,32,64,4,64]{4,3,2,1,0:T(4,128)(2,1)S(1)} %broadcast_select_fusion.2, bf16[4,64,32,64,1]{3,2,1,0,4:T(8,128)(2,1)S(1)} %dynamic-slice_bitcast_fusion.2), kind=kOutput, calls=%fused_computation.3.clone.1 | convolution fusion | flops 268435456 | bytes 13631488 | tf_op jit(solution)/shard_map/while/body/eval_jaxpr/vmap(pul,uloc->upoc)/dot_general | solution.py:87
  88.8 25.9 %fusion.62 = bf16[4,4,64,3,3,64]{5,4,2,3,1,0:T(4,128)(2,1)} fusion(bf16[4,4,64,3,3,64]{5,4,2,3,1,0:T(4,128)(2,1)} %get-tuple-element.131, s32[]{:T(128)} %get-tuple-element.130, f32[4,32,64,4,64,1]{4,2,3,1,0,5:T(8,128)} %convolution_bitcast_fusion.2, f32[4,4,32,3,3,4]{2,4,5,3,1,0:T(4,128)S(1)} %get-tuple-element.139), kind=kOutput, calls=%fused_computation.10.clone.1 | convolution fusion | flops 226639872 | bytes 17662976 | tf_op jit(solution)/shard_map/while/body/eval_jaxpr/vmap(kbje,ksij->bsie)/dot_general | solution.py:90
  114.8 2.8 gather_fusion
  117.6 12.9 %gather.11 = bf16[4,32,64,4,64]{4,3,2,1,0:T(4,128)(2,1)} reshape(bf16[128,64,256]{2,1,0:T(8,128)(2,1)} %gather_fusion) | data formatting | bytes 8388608 | tf_op jit(solution)/shard_map/while/body/eval_jaxpr/vmap(jit(_take))/gather | solution.py:84
  130.5 6.1 %broadcast_select_fusion.2 = bf16[4,32,64,4,64]{4,3,2,1,0:T(4,128)(2,1)S(1)} fusion(bf16[4,32,64,4,64]{4,3,2,1,0:T(4,128)(2,1)} %gather.11, pred[4,32]{1,0:T(4,128)(4,1)S(1)} %compare_and_fusion.2), kind=kLoop, calls=%fused_computation.5.clone.1 | loop fusion | flops 2097152 | bytes 8388736 | tf_op jit(solution)/shard_map/while/body/eval_jaxpr/vmap(jit(_take))/select_n | solution.py:84
  138.6 7.0 %convolution_bitcast_fusion.2 = f32[4,32,64,4,64,1]{4,2,3,1,0,5:T(8,128)} fusion(bf16[4,32,64,4,64]{4,3,2,1,0:T(4,128)(2,1)S(1)} %broadcast_select_fusion.2, bf16[4,64,32,64,1]{3,2,1,0,4:T(8,128)(2,1)S(1)} %dynamic-slice_bitcast_fusion.2), kind=kOutput, calls=%fused_computation.3.clone.1 | convolution fusion | flops 268435456 | bytes 13631488 | tf_op jit(solution)/shard_map/while/body/eval_jaxpr/vmap(pul,uloc->upoc)/dot_general | solution.py:87
  145.6 25.9 %fusion.62 = bf16[4,4,64,3,3,64]{5,4,2,3,1,0:T(4,128)(2,1)} fusion(bf16[4,4,64,3,3,64]{5,4,2,3,1,0:T(4,128)(2,1)} %get-tuple-element.131, s32[]{:T(128)} %get-tuple-element.130, f32[4,32,64,4,64,1]{4,2,3,1,0,5:T(8,128)} %convolution_bitcast_fusion.2, f32[4,4,32,3,3,4]{2,4,5,3,1,0:T(4,128)S(1)} %get-tuple-element.139), kind=kOutput, calls=%fused_computation.10.clone.1 | convolution fusion | flops 226639872 | bytes 17662976 | tf_op jit(solution)/shard_map/while/body/eval_jaxpr/vmap(kbje,ksij->bsie)/dot_general | solution.py:90
  171.6 2.8 gather_fusion
  174.4 12.9 %gather.11 = bf16[4,32,64,4,64]{4,3,2,1,0:T(4,128)(2,1)} reshape(bf16[128,64,256]{2,1,0:T(8,128)(2,1)} %gather_fusion) | data formatting | bytes 8388608 | tf_op jit(solution)/shard_map/while/body/eval_jaxpr/vmap(jit(_take))/gather | solution.py:84
  187.3 6.1 %broadcast_select_fusion.2 = bf16[4,32,64,4,64]{4,3,2,1,0:T(4,128)(2,1)S(1)} fusion(bf16[4,32,64,4,64]{4,3,2,1,0:T(4,128)(2,1)} %gather.11, pred[4,32]{1,0:T(4,128)(4,1)S(1)} %compare_and_fusion.2), kind=kLoop, calls=%fused_computation.5.clone.1 | loop fusion | flops 2097152 | bytes 8388736 | tf_op jit(solution)/shard_map/while/body/eval_jaxpr/vmap(jit(_take))/select_n | solution.py:84
  195.4 7.0 %convolution_bitcast_fusion.2 = f32[4,32,64,4,64,1]{4,2,3,1,0,5:T(8,128)} fusion(bf16[4,32,64,4,64]{4,3,2,1,0:T(4,128)(2,1)S(1)} %broadcast_select_fusion.2, bf16[4,64,32,64,1]{3,2,1,0,4:T(8,128)(2,1)S(1)} %dynamic-slice_bitcast_fusion.2), kind=kOutput, calls=%fused_computation.3.clone.1 | convolution fusion | flops 268435456 | bytes 13631488 | tf_op jit(solution)/shard_map/while/body/eval_jaxpr/vmap(pul,uloc->upoc)/dot_general | solution.py:87
  202.4 25.9 %fusion.62 = bf16[4,4,64,3,3,64]{5,4,2,3,1,0:T(4,128)(2,1)} fusion(bf16[4,4,64,3,3,64]{5,4,2,3,1,0:T(4,128)(2,1)} %get-tuple-element.131, s32[]{:T(128)} %get-tuple-element.130, f32[4,32,64,4,64,1]{4,2,3,1,0,5:T(8,128)} %convolution_bitcast_fusion.2, f32[4,4,32,3,3,4]{2,4,5,3,1,0:T(4,128)S(1)} %get-tuple-element.139), kind=kOutput, calls=%fused_computation.10.clone.1 | convolution fusion | flops 226639872 | bytes 17662976 | tf_op jit(solution)/shard_map/while/body/eval_jaxpr/vmap(kbje,ksij->bsie)/dot_general | solution.py:90
  228.5 2.8 gather_fusion
  231.3 12.9 %gather.11 = bf16[4,32,64,4,64]{4,3,2,1,0:T(4,128)(2,1)} reshape(bf16[128,64,256]{2,1,0:T(8,128)(2,1)} %gather_fusion) | data formatting | bytes 8388608 | tf_op jit(solution)/shard_map/while/body/eval_jaxpr/vmap(jit(_take))/gather | solution.py:84
  244.2 6.1 %broadcast_select_fusion.2 = bf16[4,32,64,4,64]{4,3,2,1,0:T(4,128)(2,1)S(1)} fusion(bf16[4,32,64,4,64]{4,3,2,1,0:T(4,128)(2,1)} %gather.11, pred[4,32]{1,0:T(4,128)(4,1)S(1)} %compare_and_fusion.2), kind=kLoop, calls=%fused_computation.5.clone.1 | loop fusion | flops 2097152 | bytes 8388736 | tf_op jit(solution)/shard_map/while/body/eval_jaxpr/vmap(jit(_take))/select_n | solution.py:84
  252.3 7.0 %convolution_bitcast_fusion.2 = f32[4,32,64,4,64,1]{4,2,3,1,0,5:T(8,128)} fusion(bf16[4,32,64,4,64]{4,3,2,1,0:T(4,128)(2,1)S(1)} %broadcast_select_fusion.2, bf16[4,64,32,64,1]{3,2,1,0,4:T(8,128)(2,1)S(1)} %dynamic-slice_bitcast_fusion.2), kind=kOutput, calls=%fused_computation.3.clone.1 | convolution fusion | flops 268435456 | bytes 13631488 | tf_op jit(solution)/shard_map/while/body/eval_jaxpr/vmap(pul,uloc->upoc)/dot_general | solution.py:87
  259.3 25.9 %fusion.62 = bf16[4,4,64,3,3,64]{5,4,2,3,1,0:T(4,128)(2,1)} fusion(bf16[4,4,64,3,3,64]{5,4,2,3,1,0:T(4,128)(2,1)} %get-tuple-element.131, s32[]{:T(128)} %get-tuple-element.130, f32[4,32,64,4,64,1]{4,2,3,1,0,5:T(8,128)} %convolution_bitcast_fusion.2, f32[4,4,32,3,3,4]{2,4,5,3,1,0:T(4,128)S(1)} %get-tuple-element.139), kind=kOutput, calls=%fused_computation.10.clone.1 | convolution fusion | flops 226639872 | bytes 17662976 | tf_op jit(solution)/shard_map/while/body/eval_jaxpr/vmap(kbje,ksij->bsie)/dot_general | solution.py:90
  285.2 7.1 %fusion.17 = f32[16,3,3,64,2,64]{5,3,4,2,1,0:T(8,128)} fusion(bf16[16,64,3,3,64,1]{4,3,1,2,0,5:T(4,128)(2,1)} %bitcast.108, bf16[16,64,2,64,1,1]{3,2,1,0,4,5:T(2,128)(2,1)} %reshape.330), kind=kOutput, calls=%fused_computation.21 | convolution fusion | flops 150994944 | bytes 6160384 | tf_op jit(solution)/shard_map/zqbld,zqbsie->zqldsie/dot_general | solution.py:103
  292.3 10.2 %copy.21 = f32[16,3,3,64,2,64]{3,0,4,2,1,5:T(8,128)} copy(f32[16,3,3,64,2,64]{5,3,4,2,1,0:T(8,128)} %fusion.17) | data formatting | bytes 9437184 | tf_op jit(solution)/shard_map/zqbld,zqbsie->zqldsie/dot_general | solution.py:103
  302.5 9.3 %fusion.19 = f32[1,3,64,3,5,64]{5,4,3,2,1,0:T(8,128)S(1)} fusion(f32[16,3,3,64,2,64]{3,0,4,2,1,5:T(8,128)} %copy.21, pred[16,2,5,3]{0,2,1,3:T(8,128)(4,1)S(1)} %copy-done.1, pred[16,2,3]{0,1,2:T(4,128)(4,1)S(1)} %copy-done.3), kind=kOutput, calls=%fused_computation.23 | convolution fusion | flops 212338080 | bytes 5456448 | tf_op jit(solution)/shard_map/zqldsie,zqluri->zudsre/dot_general | solution.py:114
  314.7 4.3 %collective-permute-start.4 = (f32[1,64,960]{1,2,0:T(8,128)S(1)}, f32[1,64,960]{1,2,0:T(8,128)S(1)}, u32[]{:S(2)}, u32[]{:S(2)}) collective-permute-start(f32[1,64,960]{1,2,0:T(8,128)S(1)} %get-tuple-element.76), channel_id=1, source_target_pairs={{0,15},{1,0},{2,1},{3,2},{4,3},{5,4},{6,5},{7,6},{8,7},{9,8},{10,9... | collective-permute-start | bytes 737288 | tf_op jit(solution)/shard_map/ppermute | solution.py:34
  318.9 6.3 %collective-permute-done.4 = f32[1,64,960]{1,2,0:T(8,128)S(1)} collective-permute-done((f32[1,64,960]{1,2,0:T(8,128)S(1)}, f32[1,64,960]{1,2,0:T(8,128)S(1)}, u32[]{:S(2)}, u32[]{:S(2)}) %collective-permute-start.4) | collective-permute-done | bytes 245792 | tf_op jit(solution)/shard_map/ppermute | solution.py:34
  325.3 3.1 collective-permute-done.5
  (65 shorter events, 23.4 us)
Async XLA Ops:
  0.0 12.6 %copy-start.2 = (s32[1,16,32]{2,1,0:T(8,128)S(1)}, s32[1,16,32]{2,1,0:T(8,128)}, u32[]{:S(2)}) copy-start(s32[1,16,32]{2,1,0:T(8,128)} %param.14) | copy-start | bytes 6148
  0.0 13.8 %copy-start.4 = (s32[1,16]{1,0:T(1,128)S(1)}, s32[1,16]{1,0:T(1,128)}, u32[]{:S(2)}) copy-start(s32[1,16]{1,0:T(1,128)} %param.15) | copy-start | bytes 196
  4.1 24.6 %collective-permute-start = (bf16[1,8,64,256]{3,2,1,0:T(8,128)(2,1)S(1)}, bf16[1,8,64,256]{3,2,1,0:T(8,128)(2,1)S(1)}, u32[]{:S(2)}, u32[]{:S(2)}) collective-permute-start(bf16[1,8,64,256]{3,2,1,0:T(8,128)(2,1)S(1)} %get-tuple-element.79), channel_id=1, source_target_pairs={{0,1},{1,2},{2,3},{3,4},{4,5},{5,6},{6,7},{7,8},{8,9},{9,10},{10,1... | collective-permute-start | bytes 786440 | tf_op jit(solution)/shard_map/ppermute | solution.py:22
  4.1 24.6 %collective-permute-start.1 = (bf16[1,8,64,256]{3,2,1,0:T(8,128)(2,1)S(1)}, bf16[1,8,64,256]{3,2,1,0:T(8,128)(2,1)S(1)}, u32[]{:S(2)}, u32[]{:S(2)}) collective-permute-start(bf16[1,8,64,256]{3,2,1,0:T(8,128)(2,1)S(1)} %get-tuple-element.78), channel_id=1, source_target_pairs={{1,0},{2,1},{3,2},{4,3},{5,4},{6,5},{7,6},{8,7},{9,8},{10,9},{11,1... | collective-permute-start | bytes 786440 | tf_op jit(solution)/shard_map/ppermute | solution.py:24
  14.6 12.9 %copy-start = (bf16[1,16,64,128]{3,2,1,0:T(8,128)(2,1)S(1)}, bf16[1,16,64,128]{3,2,1,0:T(8,128)(2,1)}, u32[]{:S(2)}) copy-start(bf16[1,16,64,128]{3,2,1,0:T(8,128)(2,1)} %param.18) | copy-start | bytes 786436
  28.7 21.2 %collective-permute-start.2 = (bf16[1,32,64,256]{3,2,1,0:T(8,128)(2,1)S(1)}, bf16[1,32,64,256]{3,2,1,0:T(8,128)(2,1)S(1)}, u32[]{:S(2)}, u32[]{:S(2)}) collective-permute-start(bf16[1,32,64,256]{3,2,1,0:T(8,128)(2,1)S(1)} %constant_dynamic-update-slice_fusion), channel_id=1, source_target_pairs={{0,16},{16,32},{32,48},{48,64},{64,80},{80,96},{96,112},{112,128},... | collective-permute-start | bytes 3145736 | tf_op jit(solution)/shard_map/ppermute | solution.py:22
  33.4 24.0 %collective-permute-start.3 = (bf16[1,32,64,256]{3,2,1,0:T(8,128)(2,1)S(1)}, bf16[1,32,64,256]{3,2,1,0:T(8,128)(2,1)S(1)}, u32[]{:S(2)}, u32[]{:S(2)}) collective-permute-start(bf16[1,32,64,256]{3,2,1,0:T(8,128)(2,1)S(1)} %constant_dynamic-update-slice_fusion), channel_id=1, source_target_pairs={{16,0},{32,16},{48,32},{64,48},{80,64},{96,80},{112,96},{128,112},... | collective-permute-start | bytes 3145736 | tf_op jit(solution)/shard_map/ppermute | solution.py:24
  292.3 10.2 %copy-start.1 = (pred[16,2,5,3]{0,2,1,3:T(8,128)(4,1)S(1)}, pred[16,2,5,3]{0,2,1,3:T(8,128)(4,1)}, u32[]{:S(2)}) copy-start(pred[16,2,5,3]{0,2,1,3:T(8,128)(4,1)} %iota_compare_fusion.2) | copy-start | bytes 1444
  292.3 10.2 %copy-start.3 = (pred[16,2,3]{0,1,2:T(4,128)(4,1)S(1)}, pred[16,2,3]{0,1,2:T(4,128)(4,1)}, u32[]{:S(2)}) copy-start(pred[16,2,3]{0,1,2:T(4,128)(4,1)} %iota_compare_fusion.4) | copy-start | bytes 292
  314.7 10.6 %collective-permute-start.4 = (f32[1,64,960]{1,2,0:T(8,128)S(1)}, f32[1,64,960]{1,2,0:T(8,128)S(1)}, u32[]{:S(2)}, u32[]{:S(2)}) collective-permute-start(f32[1,64,960]{1,2,0:T(8,128)S(1)} %get-tuple-element.76), channel_id=1, source_target_pairs={{0,15},{1,0},{2,1},{3,2},{4,3},{5,4},{6,5},{7,6},{8,7},{9,8},{10,9... | collective-permute-start | bytes 737288 | tf_op jit(solution)/shard_map/ppermute | solution.py:34
  318.9 9.5 %collective-permute-start.5 = (f32[1,64,960]{1,2,0:T(8,128)S(1)}, f32[1,64,960]{1,2,0:T(8,128)S(1)}, u32[]{:S(2)}, u32[]{:S(2)}) collective-permute-start(f32[1,64,960]{1,2,0:T(8,128)S(1)} %get-tuple-element.77), channel_id=1, source_target_pairs={{0,1},{1,2},{2,3},{3,4},{4,5},{5,6},{6,7},{7,8},{8,9},{9,10},{10,1... | collective-permute-start | bytes 737288 | tf_op jit(solution)/shard_map/ppermute | solution.py:34
where the time goes:
time: 333 us; the launch traced here: 330 us
  matrix products  149 us (45%)
  local copies, waits for them, and re-layouts  102 us (31%)
  waiting for transfers between devices  30.7 us (9%)
  other arithmetic  28.9 us (9%)
  starting transfers between devices  19.3 us (6%)
    dot_general x4, matrix products, slot_terms(): jnp.einsum('kbje,ksij->bsie', triple_product, slot_place, precision=lax.P...  104 us
    gather x8, local copies, waits for them, and re-layouts, slot_terms(): jnp.take(flat_rows, slot_rows, axis=0)  62.8 us
    dot_general x4, matrix products, slot_terms(): jnp.einsum('pul,uloc->upoc', coupling_weight, selected_entries, preferred...  28.1 us
    select_n x8, other arithmetic, slot_terms(): jnp.take(flat_rows, slot_rows, axis=0)  24.5 us
    ppermute x2, waiting for transfers between devices, with_halo(): lax.ppermute(tail, axis, [(i, (i + 1) % count) for i in range(ends)])  13.8 us
    reshape x1, local copies, waits for them, and re-layouts, body(): a_vals.reshape((turns_rows, group_rows, block_size, slot_count, block_size))  12.9 us
    ppermute x2, starting transfers between devices, with_halo(): lax.ppermute(head, axis, [((i + 1) % count, i) for i in range(ends)])  10.4 us
    dot_general x1, local copies, waits for them, and re-layouts, body(): jnp.einsum('zqbld,zqbsie->zqldsie', restrict, fine_rows, preferred_elemen...  10.2 us
  transfers between devices with their start and end apart: 6, of which 4 were waited for; matrix products, arithmetic and copies ran while one was open for 5% of the time, Pallas kernels for 0%

commit v1 on v0

v1 whole, which is shorter than its diff:
```python
import jax
import jax.numpy as jnp
from jax import lax
from jax.experimental import pallas as pl
from jax.experimental.pallas import tpu as pltpu
from jax.sharding import PartitionSpec as P

PLANE = 256
AGG = 16
HALF = 8
B = 64
KA = 32
PAIR = 2 * B
TILES = KA // 2
EMPTY = 2 * TILES
SPAN = 24
DEPTH = HALF * B

F32 = jnp.float32
BF16 = jnp.bfloat16


def shift_cols(value, step):
    count = lax.axis_size("col")
    return lax.ppermute(value, "col", [(i, (i + step) % count) for i in range(count)])


def swap_rows(value, first):
    pairs = []
    for row in range(first, lax.axis_size("row") - 1, 2):
        pairs += [(row, row + 1), (row + 1, row)]
    return lax.ppermute(value, "row", pairs)


def plane_of(first):
    return 2 * lax.rem(lax.axis_index("row") + first + 1, 2)


def swap_lanes(x):
    return pltpu.roll(x, B, 1)


def flip_mask(cols_ref, q):
    first_own = cols_ref[0:1, q : q + 1] == lax.axis_index("col")
    value = jnp.where(first_own, 1.0, 0.0) if q < HALF else jnp.where(first_own, 0.0, 1.0)
    return jnp.broadcast_to(value, (B, PAIR)) > 0.5


def ordered(x, cols_ref, q):
    return jnp.where(flip_mask(cols_ref, q), swap_lanes(x), x)


def order_kernel(cols_hbm, p_hbm, all_ref, head_ref, tail_ref, cols_ref, raw, sems):
    parts = 4
    size = AGG // parts
    cols_copy = pltpu.make_async_copy(cols_hbm, cols_ref, sems.at[parts])
    cols_copy.start()

    def fetch(part):
        at = pl.ds(part * size, size)
        return pltpu.make_async_copy(p_hbm.at[0, at], raw.at[at], sems.at[part])

    for part in range(parts):
        fetch(part).start()
    cols_copy.wait()
    for part in range(parts):
        fetch(part).wait()
        for q in range(part * size, (part + 1) * size):
            y = ordered(raw[q], cols_ref, q)
            all_ref[q] = y
            if q < HALF:
                head_ref[q] = y
            else:
                tail_ref[q - HALF] = y


def order(p_vals, p_cols):
    half = jax.ShapeDtypeStruct((HALF, B, PAIR), BF16)
    return pl.pallas_call(
        order_kernel,
        out_shape=(jax.ShapeDtypeStruct((AGG, B, PAIR), BF16), half, half),
        in_specs=[pl.BlockSpec(memory_space=pl.ANY)] * 2,
        out_specs=tuple(whole(3)),
        scratch_shapes=[
            pltpu.VMEM((2, AGG), jnp.int32),
            pltpu.VMEM((AGG, B, PAIR), BF16),
            pltpu.SemaphoreType.DMA((5,)),
        ],
        compiler_params=pltpu.CompilerParams(vmem_limit_bytes=4 << 20),
        name="order",
    )(in_hbm(p_cols[0].T), in_hbm(p_vals))


def prepare_kernel(cols_hbm, a_hbm, r_hbm, slots_ref, restrict_ref, cols_ref, raw, sems, r_sem, cols_sem):
    def fetch(q):
        return pltpu.make_async_copy(a_hbm.at[0, q], slots_ref.at[q, :, pl.ds(0, KA * B)], sems.at[q])

    for q in range(AGG):
        fetch(q).start()
    r_copy = pltpu.make_async_copy(r_hbm.at[0], raw, r_sem)
    r_copy.start()
    cols_copy = pltpu.make_async_copy(cols_hbm, cols_ref, cols_sem)
    cols_copy.start()

    def row(q, carry):
        slots_ref[q, :, EMPTY * PAIR :] = jnp.zeros((B, PAIR), BF16)
        fetch(q).wait()
        for k in range(TILES):
            x = slots_ref[q, :, k * PAIR : (k + 1) * PAIR]
            slots_ref[q, :, (TILES + k) * PAIR : (TILES + k + 1) * PAIR] = swap_lanes(x)
        return carry

    lax.fori_loop(0, AGG, row, 0)
    r_copy.wait()
    cols_copy.wait()
    for q in range(0, AGG, 2):
        two = jnp.concatenate([ordered(raw[q], cols_ref, q), ordered(raw[q + 1], cols_ref, q + 1)], axis=0)
        at = (q % HALF) * B
        restrict_ref[q // HALF, :, at : at + PAIR] = two.T


def prepare(r_cols, a_vals, r_vals):
    return pl.pallas_call(
        prepare_kernel,
        out_shape=(
            pltpu.VMEM((AGG, B, (EMPTY + 1) * PAIR), BF16),
            jax.ShapeDtypeStruct((2, PAIR, DEPTH), BF16),
        ),
        in_specs=[pl.BlockSpec(memory_space=pl.ANY)] * 3,
        out_specs=tuple(whole(2)),
        scratch_shapes=[
            pltpu.VMEM((2, AGG), jnp.int32),
            pltpu.VMEM((AGG, B, PAIR), BF16),
            pltpu.SemaphoreType.DMA((AGG,)),
            pltpu.SemaphoreType.DMA,
            pltpu.SemaphoreType.DMA,
        ],
        compiler_params=pltpu.CompilerParams(vmem_limit_bytes=12 << 20),
        cost_estimate=pl.CostEstimate(flops=0, bytes_accessed=6 << 20, transcendentals=0),
        name="prepare",
    )(
        in_hbm(r_cols[0].T),
        in_hbm(a_vals),
        in_hbm(r_vals),
    )


def placed(x, shifted):
    if not shifted:
        return x
    lower = lax.broadcasted_iota(jnp.int32, (B, PAIR), 1) < B
    first, second = swap_lanes(x[:, :PAIR]), swap_lanes(x[:, PAIR:])
    return jnp.concatenate([jnp.where(lower, 0.0, first), jnp.where(lower, first, second)], axis=1)


def merged(low, high):
    lower = lax.broadcasted_iota(jnp.int32, (DEPTH, PAIR), 1) < B
    high = swap_lanes(high)
    return low + jnp.where(lower, 0.0, high), jnp.where(lower, high, 0.0)


def rows_of(ref, start):
    return ref[start : start + HALF].reshape(DEPTH, PAIR)


def gather(index_ref, slots_ref, s, half, j, into):
    lower = lax.broadcasted_iota(jnp.int32, (B, PAIR), 1) < B
    for e in range(HALF):
        q = half * HALF + e
        at = q * (3 * SPAN) + s * SPAN + j * HALF
        for tile in range(HALF // 2):
            rows, cols = slice(e * B, (e + 1) * B), slice(tile * PAIR, (tile + 1) * PAIR)
            if (j == 0 and tile < e // 2) or (j == 2 and tile > e // 2):
                into[rows, cols] = jnp.zeros((B, PAIR), BF16)
                continue
            first = pl.multiple_of(index_ref[at + 2 * tile] * PAIR, PAIR)
            second = pl.multiple_of(index_ref[at + 2 * tile + 1] * PAIR, PAIR)
            into[rows, cols] = jnp.where(
                lower, slots_ref[q, :, pl.ds(first, PAIR)], slots_ref[q, :, pl.ds(second, PAIR)]
            )


def middle_kernel(
    index_ref, slots_ref, restrict_ref, left_ref, own_ref, right_ref, own_out, before_out, after_out, band
):
    parts = [(left_ref, 0), (own_ref, 0), (own_ref, HALF), (right_ref, 0)]
    terms = []
    turn = 0
    for half in range(2):
        sums = [None, None]
        for j in range(3):
            turn = (turn + 1) % 3
            gather(index_ref, slots_ref, 1, half, j, band.at[turn])
            term = jnp.dot(band[turn], rows_of(*parts[half + j]), preferred_element_type=F32)
            side = (half + j) // 2
            sums[side] = term if sums[side] is None else sums[side] + term
        first, second = merged(*sums)
        fine = jnp.concatenate([first.astype(BF16), second.astype(BF16)], axis=1)
        terms.append(jnp.dot(restrict_ref[half], fine, preferred_element_type=F32))
    own_out[...] = terms[0][B:] + terms[1][:B]
    before_out[...] = placed(terms[0][:B], True).astype(BF16)
    after_out[...] = placed(terms[1][B:], True).astype(BF16)


def inner_kernel(index_ref, slots_ref, odd_ref, even_ref, edge_ref, sums_ref, band):
    turn = 0
    for n, near in enumerate((odd_ref, even_ref)):
        s = plane_of(1 - n)
        for half in range(2):
            sums = [None, None]
            for j in range(3):
                part = half + j
                if part in (0, 3):
                    gather(index_ref, slots_ref, s, half, j, edge_ref.at[2 * n + half])
                    continue
                turn = (turn + 1) % 3
                gather(index_ref, slots_ref, s, half, j, band.at[turn])
                sums[part // 2] = jnp.dot(
                    band[turn], rows_of(near, (part - 1) * HALF), preferred_element_type=F32
                )
            first, second = merged(*sums)
            sums_ref[n, half, :, :PAIR] = first
            sums_ref[n, half, :, PAIR:] = second


def outer_kernel(
    edge_ref, sums_ref, restrict_ref, left_ref, right_ref, own_mid, before_mid, after_mid,
    own_ref, before_ref, after_ref
):
    lower = lax.broadcasted_iota(jnp.int32, (DEPTH, PAIR), 1) < B
    mid = slice(2 * PAIR, 4 * PAIR)
    own_ref[:, mid] = own_mid[...]
    before_ref[:, mid] = before_mid[...]
    after_ref[:, mid] = after_mid[...]
    for n in range(2):
        terms = []
        for half in range(2):
            first, second = sums_ref[n, half, :, :PAIR], sums_ref[n, half, :, PAIR:]
            against = rows_of(right_ref if half else left_ref, n * HALF)
            if half:
                against = swap_lanes(against)
            term = jnp.dot(edge_ref[2 * n + half], against, preferred_element_type=F32)
            if half:
                first = first + jnp.where(lower, 0.0, term)
                second = second + jnp.where(lower, term, 0.0)
            else:
                first = first + term
            fine = jnp.concatenate([first.astype(BF16), second.astype(BF16)], axis=1)
            terms.append(jnp.dot(restrict_ref[half], fine, preferred_element_type=F32))
        cols = pl.ds(pl.multiple_of(plane_of(1 - n) * 2 * PAIR, PAIR), 2 * PAIR)
        own_ref[:, cols] = placed(terms[0][B:] + terms[1][:B], True)
        before_ref[:, cols] = terms[0][:B].astype(BF16)
        after_ref[:, cols] = terms[1][B:].astype(BF16)


OWN_AT = (0, 1, 3, 4, 5, 6)
ABOVE_AT = (1, 2, 3, 4, 6, 7)
BELOW_AT = (0, 1, 2, 3, 5, 6)


def join_kernel(own_ref, above_ref, below_ref, out_ref):
    for tile in range(8):
        width = PAIR if tile < 7 else B
        total = None
        for ref, places in ((own_ref, OWN_AT), (above_ref, ABOVE_AT), (below_ref, BELOW_AT)):
            if tile in places:
                at = places.index(tile) * PAIR
                piece = ref[:, at : at + width].astype(F32)
                total = piece if total is None else total + piece
        out_ref[0, :, tile * PAIR : tile * PAIR + width] = total


def in_hbm(x):
    return pltpu.with_memory_space_constraint(x, pltpu.HBM)


def whole(count):
    return [pl.BlockSpec(memory_space=pltpu.VMEM)] * count


def slot_table(a_cols, a_count):
    first_block = lax.axis_index("col") * AGG
    local_q = jnp.arange(AGG, dtype=jnp.int32)[:, None]
    reach = (a_cols[0] % PLANE - first_block + HALF) % PLANE - HALF * (local_q // HALF)
    place = a_cols[0] // PLANE * SPAN + reach
    slot = jnp.arange(KA, dtype=jnp.int32)
    live = slot[None, :] < a_count[0][:, None]
    dest = jnp.arange(3 * SPAN, dtype=jnp.int32)
    hit = (place[:, :, None] == dest) & live[:, :, None]
    entry = slot[:, None] // 2 + TILES * ((slot[:, None] + dest[None, :]) % 2)
    return EMPTY + jnp.sum(jnp.where(hit, entry[None] - EMPTY, 0), axis=1)


def body(a_vals, a_cols, a_count, p_vals, p_cols, r_vals, r_cols):
    own, head, tail = order(p_vals, p_cols)
    odd = swap_rows(own, 1)
    even = swap_rows(own, 0)
    left = shift_cols(tail, 1)
    right = shift_cols(head, -1)
    index = slot_table(a_cols, a_count).reshape(-1)
    slots, restrict = prepare(r_cols, a_vals, r_vals)
    odd, even, left, right, restrict, index = lax.optimization_barrier((odd, even, left, right, restrict, index))
    smem = pl.BlockSpec(memory_space=pltpu.SMEM)
    band = pltpu.VMEM((3, DEPTH, DEPTH), BF16)
    own_mid, before_mid, after_mid = pl.pallas_call(
        middle_kernel,
        out_shape=(
            jax.ShapeDtypeStruct((B, 2 * PAIR), F32),
            jax.ShapeDtypeStruct((B, 2 * PAIR), BF16),
            jax.ShapeDtypeStruct((B, 2 * PAIR), BF16),
        ),
        in_specs=[smem] + whole(5),
        out_specs=tuple(whole(3)),
        scratch_shapes=[band],
        compiler_params=pltpu.CompilerParams(vmem_limit_bytes=16 << 20),
        cost_estimate=pl.CostEstimate(flops=1 << 30, bytes_accessed=4 << 20, transcendentals=0),
        name="middle",
    )(index, slots, restrict, left, own, right)
    both_left = shift_cols(jnp.concatenate([odd[HALF:], even[HALF:]], axis=0), 1)
    both_right = shift_cols(jnp.concatenate([odd[:HALF], even[:HALF]], axis=0), -1)

    edge, sums = pl.pallas_call(
        inner_kernel,
        out_shape=(
            jax.ShapeDtypeStruct((4, DEPTH, DEPTH), BF16),
            jax.ShapeDtypeStruct((2, 2, DEPTH, 2 * PAIR), F32),
        ),
        in_specs=[smem] + whole(3),
        out_specs=tuple(whole(2)),
        scratch_shapes=[band],
        compiler_params=pltpu.CompilerParams(vmem_limit_bytes=16 << 20),
        cost_estimate=pl.CostEstimate(flops=1 << 30, bytes_accessed=8 << 20, transcendentals=0),
        name="inner",
    )(index, slots, odd, even)
    owned, before, after = pl.pallas_call(
        outer_kernel,
        out_shape=(
            jax.ShapeDtypeStruct((B, 6 * PAIR), F32),
            jax.ShapeDtypeStruct((B, 6 * PAIR), BF16),
            jax.ShapeDtypeStruct((B, 6 * PAIR), BF16),
        ),
        in_specs=whole(8),
        out_specs=tuple(whole(3)),
        compiler_params=pltpu.CompilerParams(vmem_limit_bytes=12 << 20),
        cost_estimate=pl.CostEstimate(flops=1 << 30, bytes_accessed=4 << 20, transcendentals=0),
        name="outer",
    )(edge, sums, restrict, both_left, both_right, own_mid, before_mid, after_mid)
    above = shift_cols(before, -1)
    below = shift_cols(after, 1)
    return pl.pallas_call(
        join_kernel,
        out_shape=jax.ShapeDtypeStruct((1, B, 15 * B), F32),
        in_specs=whole(3),
        out_specs=whole(1)[0],
        compiler_params=pltpu.CompilerParams(vmem_limit_bytes=4 << 20),
        name="join",
    )(owned, above, below)


def solution(mesh):
    return jax.shard_map(
        body,
        mesh=mesh,
        in_specs=(
            P("row", "col", None, None),
            P("row", "col", None),
            P("row", "col"),
            P("row", "col", None, None),
            P("row", "col", None),
            P("row", "col", None, None),
            P("row", "col", None),
        ),
        out_specs=P("row", "col", None),
        check_vma=False,
    )
```

time: 333 us -> 41.1 us (0.12)
  the two profiles are of different devices: /device:TPU:30 before, /device:TPU:40 now
where the time goes in v1:
time: 41.1 us; the launch traced here: 40.9 us
  starting transfers between devices  20 us (49%)
  Pallas kernels  13.4 us (33%)
  waiting for transfers between devices  5.26 us (13%)
  other arithmetic  1.85 us (5%)
    ppermute x6, starting transfers between devices, shift_cols(): lax.ppermute(value, 'col', [(i, (i + step) % count) for i in range(count)])  11.8 us
    ppermute x2, starting transfers between devices, swap_rows(): return lax.ppermute(value, 'row', pairs)  8.19 us
    ppermute x6, waiting for transfers between devices, shift_cols(): lax.ppermute(value, 'col', [(i, (i + step) % count) for i in range(count)])  5.26 us
    pallas_call x1, Pallas kernels, prepare(): pl.pallas_call(prepare_kernel, out_shape=(pltpu.VMEM((AGG, B, (EMPTY + 1)...  3.67 us
    pallas_call x1, Pallas kernels, body(): pl.pallas_call(inner_kernel, out_shape=(jax.ShapeDtypeStruct((4, DEPTH, D...  3.16 us
    pallas_call x1, Pallas kernels, body(): pl.pallas_call(middle_kernel, out_shape=(jax.ShapeDtypeStruct((B, 2 * PAI...  2.92 us
    pallas_call x1, Pallas kernels, body(): pl.pallas_call(outer_kernel, out_shape=(jax.ShapeDtypeStruct((B, 6 * PAIR...  1.56 us
    pallas_call x1, Pallas kernels, order(): pl.pallas_call(order_kernel, out_shape=(jax.ShapeDtypeStruct((AGG, B, PAI...  1.39 us
  transfers between devices with their start and end apart: 8, of which 2 were waited for; matrix products, arithmetic and copies ran while one was open for 5% of the time, Pallas kernels for 24%

profile of v1, /device:TPU:40, one launch (start us, length us, event | category | flops | bytes accessed | tf_op | source)
XLA Modules:
  0.0 40.9 jit_solution(9066013880659940250)
XLA Ops:
  0.0 1.4 %order.1 = (bf16[16,64,128]{2,1,0:T(8,128)(2,1)S(1)}, bf16[8,64,128]{2,1,0:T(8,128)(2,1)S(1)}, bf16[8,64,128]{2,1,0:T(8,128)(2,1)S(1)}) custom-call(s32[2,16]{1,0:T(2,128)} %bitcast.23, bf16[1,16,64,128]{3,2,1,0:T(8,128)(2,1)} %p_hbm.1), custom_call_target="tpu_custom_call" | custom-call | tf_op jit(solution)/shard_map/order/pallas_call | solution.py:79
  1.4 3.4 %collective-permute-start.1 = (bf16[16,64,128]{2,1,0:T(8,128)(2,1)S(1)}, bf16[16,64,128]{2,1,0:T(8,128)(2,1)S(1)}, u32[]{:S(2)}, u32[]{:S(2)}) collective-permute-start(bf16[16,64,128]{2,1,0:T(8,128)(2,1)S(1)} %get-tuple-element.24.own_ref), channel_id=1, source_target_pairs={{0,16},{16,0},{32,48},{48,32},{64,80},{80,64},{96,112},{112,96},{1... | collective-permute-start | bytes 786440 | tf_op jit(solution)/shard_map/ppermute | solution.py:32
  4.8 4.8 %collective-permute-start = (bf16[16,64,128]{2,1,0:T(8,128)(2,1)S(1)}, bf16[16,64,128]{2,1,0:T(8,128)(2,1)S(1)}, u32[]{:S(2)}, u32[]{:S(2)}) collective-permute-start(bf16[16,64,128]{2,1,0:T(8,128)(2,1)S(1)} %get-tuple-element.24.own_ref), channel_id=1, source_target_pairs={{16,32},{32,16},{48,64},{64,48},{80,96},{96,80},{112,128},{128,112... | collective-permute-start | bytes 786440 | tf_op jit(solution)/shard_map/ppermute | solution.py:32
  9.6 0.0 collective-permute-start.2
  9.6 7.9 %collective-permute-start.3 = (bf16[8,64,128]{2,1,0:T(8,128)(2,1)S(1)}, bf16[8,64,128]{2,1,0:T(8,128)(2,1)S(1)}, u32[]{:S(2)}, u32[]{:S(2)}) collective-permute-start(bf16[8,64,128]{2,1,0:T(8,128)(2,1)S(1)} %get-tuple-element.26), channel_id=1, source_target_pairs={{0,15},{1,0},{2,1},{3,2},{4,3},{5,4},{6,5},{7,6},{8,7},{9,8},{10,9... | collective-permute-start | bytes 393224 | tf_op jit(solution)/shard_map/ppermute | solution.py:25
  17.6 0.7 %iota_compare_fusion.1 = pred[16,32]{1,0:T(8,128)(4,1)S(1)} fusion(s32[16]{0:T(128)} %bitcast.25), kind=kLoop, calls=%fused_computation.32 | loop fusion | flops 512 | bytes 576 | tf_op jit(solution)/shard_map/lt | solution.py:287
  18.3 0.1 fusion.4
  18.4 0.8 %fusion.9 = s32[16,32]{1,0:T(8,128)S(1)} fusion(s32[1,16,32]{2,1,0:T(8,128)} %param.8, s32[16]{0:T(128)S(1)} %fusion.17, s32[]{:T(128)S(6)} %mul.33), kind=kLoop, calls=%fused_computation.24 | loop fusion | flops 17920 | bytes 4164 | tf_op jit(solution)/shard_map/add | solution.py:285
  19.1 0.2 select_reduce_fusion
  19.4 0.1 add.117.index_ref
  19.5 3.7 %prepare.1 = (bf16[16,64,4224]{2,1,0:T(8,128)(2,1)S(1)}, bf16[2,128,512]{2,1,0:T(8,128)(2,1)S(1)}) custom-call(s32[2,16]{1,0:T(2,128)} %bitcast.24, bf16[1,16,64,2048]{3,2,1,0:T(8,128)(2,1)} %a_hbm.1, bf16[1,16,64,128]{3,2,1,0:T(8,128)(2,1)} %r_hbm.1), custom_call_target="tpu_custom_call" | custom-call | bytes 6291456 | tf_op jit(solution)/shard_map/prepare/pallas_call | solution.py:123
  23.1 0.0 collective-permute-done.2.left_ref
  23.2 0.0 collective-permute-done.3.right_ref
  23.2 0.0 collective-permute-done.1.even_ref
  23.2 0.0 collective-permute-done.odd_ref
  23.3 0.0 collective-permute-start.4
  23.3 2.9 %collective-permute-start.5 = (bf16[16,64,128]{2,1,0:T(8,128)(2,1)S(1)}, bf16[16,64,128]{2,1,0:T(8,128)(2,1)S(1)}, u32[]{:S(2)}, u32[]{:S(2)}) collective-permute-start(bf16[16,64,128]{2,1,0:T(8,128)(2,1)S(1)} %pad_maximum_fusion.1), channel_id=1, source_target_pairs={{0,15},{1,0},{2,1},{3,2},{4,3},{5,4},{6,5},{7,6},{8,7},{9,8},{10,9... | collective-permute-start | bytes 786440 | tf_op jit(solution)/shard_map/ppermute | solution.py:25
  26.3 3.2 %inner.1 = (bf16[4,512,512]{2,1,0:T(8,128)(2,1)S(1)}, f32[2,2,512,256]{3,2,1,0:T(8,128)S(1)}) custom-call(s32[1152]{0:T(1024)S(1)} %add.117.index_ref, bf16[16,64,4224]{2,1,0:T(8,128)(2,1)S(1)} %get-tuple-element.29.slots_ref, bf16[16,64,128]{2,1,0:T(8,128)(2,1)S(1)} %collective-permute-done.odd_ref, bf16[16,64,128]{2,1,0:T(8,128)(2,1)S(1)} %collective-permute-done.1.even_ref), custom_call_target="tpu_custom_call" | custom-call | flops 1073741824 | bytes 8388608 | tf_op jit(solution)/shard_map/inner/pallas_call | solution.py:322
  29.4 2.9 %middle.1 = (f32[64,256]{1,0:T(8,128)S(1)}, bf16[64,256]{1,0:T(8,128)(2,1)S(1)}, bf16[64,256]{1,0:T(8,128)(2,1)S(1)}) custom-call(s32[1152]{0:T(1024)S(1)} %add.117.index_ref, bf16[16,64,4224]{2,1,0:T(8,128)(2,1)S(1)} %get-tuple-element.29.slots_ref, bf16[2,128,512]{2,1,0:T(8,128)(2,1)S(1)} %get-tuple-element.34.restrict_ref, ...), custom_call_target="tpu_custom_call" | custom-call | flops 1073741824 | bytes 4194304 | tf_op jit(solution)/shard_map/middle/pallas_call | solution.py:305
  32.4 0.0 collective-permute-done.4.left_ref
  32.4 0.0 collective-permute-done.5.right_ref
  32.4 1.6 %outer.1 = (f32[64,768]{1,0:T(8,128)S(1)}, bf16[64,768]{1,0:T(8,128)(2,1)S(1)}, bf16[64,768]{1,0:T(8,128)(2,1)S(1)}) custom-call(bf16[4,512,512]{2,1,0:T(8,128)(2,1)S(1)} %get-tuple-element.32.edge_ref, f32[2,2,512,256]{3,2,1,0:T(8,128)S(1)} %get-tuple-element.33.sums_ref, bf16[2,128,512]{2,1,0:T(8,128)(2,1)S(1)} %get-tuple-element.34.restrict_ref, ...), custom_call_target="tpu_custom_call" | custom-call | flops 1073741824 | bytes 4194304 | tf_op jit(solution)/shard_map/outer/pallas_call | solution.py:335
  34.0 0.9 %collective-permute-start.6 = (bf16[64,768]{1,0:T(8,128)(2,1)S(1)}, bf16[64,768]{1,0:T(8,128)(2,1)S(1)}, u32[]{:S(2)}, u32[]{:S(2)}) collective-permute-start(bf16[64,768]{1,0:T(8,128)(2,1)S(1)} %get-tuple-element.41), channel_id=1, source_target_pairs={{0,15},{1,0},{2,1},{3,2},{4,3},{5,4},{6,5},{7,6},{8,7},{9,8},{10,9... | collective-permute-start | bytes 294920 | tf_op jit(solution)/shard_map/ppermute | solution.py:25
  34.9 0.0 collective-permute-start.7
  34.9 2.2 %collective-permute-done.6.above_ref = bf16[64,768]{1,0:T(8,128)(2,1)S(1)} collective-permute-done((bf16[64,768]{1,0:T(8,128)(2,1)S(1)}, bf16[64,768]{1,0:T(8,128)(2,1)S(1)}, u32[]{:S(2)}, u32[]{:S(2)}) %collective-permute-start.6) | collective-permute-done | bytes 98336 | tf_op jit(solution)/shard_map/ppermute | solution.py:25
  37.1 3.0 %collective-permute-done.7.below_ref = bf16[64,768]{1,0:T(8,128)(2,1)S(1)} collective-permute-done((bf16[64,768]{1,0:T(8,128)(2,1)S(1)}, bf16[64,768]{1,0:T(8,128)(2,1)S(1)}, u32[]{:S(2)}, u32[]{:S(2)}) %collective-permute-start.7) | collective-permute-done | bytes 98336 | tf_op jit(solution)/shard_map/ppermute | solution.py:25
  40.1 0.7 %join.1 = f32[1,64,960]{2,1,0:T(8,128)} custom-call(f32[64,768]{1,0:T(8,128)S(1)} %get-tuple-element.40.own_ref, bf16[64,768]{1,0:T(8,128)(2,1)S(1)} %collective-permute-done.6.above_ref, bf16[64,768]{1,0:T(8,128)(2,1)S(1)} %collective-permute-done.7.below_ref), custom_call_target="tpu_custom_call" | custom-call | tf_op jit(solution)/shard_map/join/pallas_call | solution.py:350
  (6 shorter events, 0.1 us)
Async XLA Ops:
  1.4 21.8 %collective-permute-start.1 = (bf16[16,64,128]{2,1,0:T(8,128)(2,1)S(1)}, bf16[16,64,128]{2,1,0:T(8,128)(2,1)S(1)}, u32[]{:S(2)}, u32[]{:S(2)}) collective-permute-start(bf16[16,64,128]{2,1,0:T(8,128)(2,1)S(1)} %get-tuple-element.24.own_ref), channel_id=1, source_target_pairs={{0,16},{16,0},{32,48},{48,32},{64,80},{80,64},{96,112},{112,96},{1... | collective-permute-start | bytes 786440 | tf_op jit(solution)/shard_map/ppermute | solution.py:32
  4.8 18.4 %collective-permute-start = (bf16[16,64,128]{2,1,0:T(8,128)(2,1)S(1)}, bf16[16,64,128]{2,1,0:T(8,128)(2,1)S(1)}, u32[]{:S(2)}, u32[]{:S(2)}) collective-permute-start(bf16[16,64,128]{2,1,0:T(8,128)(2,1)S(1)} %get-tuple-element.24.own_ref), channel_id=1, source_target_pairs={{16,32},{32,16},{48,64},{64,48},{80,96},{96,80},{112,128},{128,112... | collective-permute-start | bytes 786440 | tf_op jit(solution)/shard_map/ppermute | solution.py:32
  9.6 13.5 %collective-permute-start.2 = (bf16[8,64,128]{2,1,0:T(8,128)(2,1)S(1)}, bf16[8,64,128]{2,1,0:T(8,128)(2,1)S(1)}, u32[]{:S(2)}, u32[]{:S(2)}) collective-permute-start(bf16[8,64,128]{2,1,0:T(8,128)(2,1)S(1)} %get-tuple-element.25), channel_id=1, source_target_pairs={{0,1},{1,2},{2,3},{3,4},{4,5},{5,6},{6,7},{7,8},{8,9},{9,10},{10,1... | collective-permute-start | bytes 393224 | tf_op jit(solution)/shard_map/ppermute | solution.py:25
  9.6 13.5 %collective-permute-start.3 = (bf16[8,64,128]{2,1,0:T(8,128)(2,1)S(1)}, bf16[8,64,128]{2,1,0:T(8,128)(2,1)S(1)}, u32[]{:S(2)}, u32[]{:S(2)}) collective-permute-start(bf16[8,64,128]{2,1,0:T(8,128)(2,1)S(1)} %get-tuple-element.26), channel_id=1, source_target_pairs={{0,15},{1,0},{2,1},{3,2},{4,3},{5,4},{6,5},{7,6},{8,7},{9,8},{10,9... | collective-permute-start | bytes 393224 | tf_op jit(solution)/shard_map/ppermute | solution.py:25
  23.3 9.1 %collective-permute-start.4 = (bf16[16,64,128]{2,1,0:T(8,128)(2,1)S(1)}, bf16[16,64,128]{2,1,0:T(8,128)(2,1)S(1)}, u32[]{:S(2)}, u32[]{:S(2)}) collective-permute-start(bf16[16,64,128]{2,1,0:T(8,128)(2,1)S(1)} %pad_maximum_fusion), channel_id=1, source_target_pairs={{0,1},{1,2},{2,3},{3,4},{4,5},{5,6},{6,7},{7,8},{8,9},{9,10},{10,1... | collective-permute-start | bytes 786440 | tf_op jit(solution)/shard_map/ppermute | solution.py:25
  23.3 9.1 %collective-permute-start.5 = (bf16[16,64,128]{2,1,0:T(8,128)(2,1)S(1)}, bf16[16,64,128]{2,1,0:T(8,128)(2,1)S(1)}, u32[]{:S(2)}, u32[]{:S(2)}) collective-permute-start(bf16[16,64,128]{2,1,0:T(8,128)(2,1)S(1)} %pad_maximum_fusion.1), channel_id=1, source_target_pairs={{0,15},{1,0},{2,1},{3,2},{4,3},{5,4},{6,5},{7,6},{8,7},{9,8},{10,9... | collective-permute-start | bytes 786440 | tf_op jit(solution)/shard_map/ppermute | solution.py:25
  34.0 3.1 %collective-permute-start.6 = (bf16[64,768]{1,0:T(8,128)(2,1)S(1)}, bf16[64,768]{1,0:T(8,128)(2,1)S(1)}, u32[]{:S(2)}, u32[]{:S(2)}) collective-permute-start(bf16[64,768]{1,0:T(8,128)(2,1)S(1)} %get-tuple-element.41), channel_id=1, source_target_pairs={{0,15},{1,0},{2,1},{3,2},{4,3},{5,4},{6,5},{7,6},{8,7},{9,8},{10,9... | collective-permute-start | bytes 294920 | tf_op jit(solution)/shard_map/ppermute | solution.py:25
  34.9 5.3 %collective-permute-start.7 = (bf16[64,768]{1,0:T(8,128)(2,1)S(1)}, bf16[64,768]{1,0:T(8,128)(2,1)S(1)}, u32[]{:S(2)}, u32[]{:S(2)}) collective-permute-start(bf16[64,768]{1,0:T(8,128)(2,1)S(1)} %get-tuple-element.42), channel_id=1, source_target_pairs={{0,1},{1,2},{2,3},{3,4},{4,5},{5,6},{6,7},{7,8},{8,9},{9,10},{10,1... | collective-permute-start | bytes 294920 | tf_op jit(solution)/shard_map/ppermute | solution.py:25

commit v2 on v1

v2 whole, which is shorter than its diff:
```python
import jax
import jax.numpy as jnp
from jax import lax
from jax.experimental import pallas as pl
from jax.experimental.pallas import tpu as pltpu
from jax.sharding import PartitionSpec as P

PLANE = 256
AGG = 16
HALF = 8
B = 64
KA = 32
PAIR = 2 * B
TILES = KA // 2
EMPTY = 2 * TILES
SPAN = 24
DEPTH = HALF * B

F32 = jnp.float32
BF16 = jnp.bfloat16


def shift_cols(value, step):
    count = lax.axis_size("col")
    return lax.ppermute(value, "col", [(i, (i + step) % count) for i in range(count)])


def swap_rows(value, first):
    pairs = []
    for row in range(first, lax.axis_size("row") - 1, 2):
        pairs += [(row, row + 1), (row + 1, row)]
    return lax.ppermute(value, "row", pairs)


def plane_of(first):
    return 2 * lax.rem(lax.axis_index("row") + first + 1, 2)


def swap_lanes(x):
    return pltpu.roll(x, B, 1)


def flip_mask(cols_ref, q):
    first_own = cols_ref[0:1, q : q + 1] == lax.axis_index("col")
    value = jnp.where(first_own, 1.0, 0.0) if q < HALF else jnp.where(first_own, 0.0, 1.0)
    return jnp.broadcast_to(value, (B, PAIR)) > 0.5


def ordered(x, cols_ref, q):
    return jnp.where(flip_mask(cols_ref, q), swap_lanes(x), x)


def order_kernel(cols_hbm, p_hbm, all_ref, head_ref, tail_ref, cols_ref, raw, sems):
    parts = 4
    size = AGG // parts
    cols_copy = pltpu.make_async_copy(cols_hbm, cols_ref, sems.at[parts])
    cols_copy.start()

    def fetch(part):
        at = pl.ds(part * size, size)
        return pltpu.make_async_copy(p_hbm.at[0, at], raw.at[at], sems.at[part])

    for part in range(parts):
        fetch(part).start()
    cols_copy.wait()
    for part in range(parts):
        fetch(part).wait()
        for q in range(part * size, (part + 1) * size):
            y = ordered(raw[q], cols_ref, q)
            all_ref[q] = y
            if q < HALF:
                head_ref[q] = y
            else:
                tail_ref[q - HALF] = y


def order(p_vals, p_cols):
    half = jax.ShapeDtypeStruct((HALF, B, PAIR), BF16)
    return pl.pallas_call(
        order_kernel,
        out_shape=(jax.ShapeDtypeStruct((AGG, B, PAIR), BF16), half, half),
        in_specs=[pl.BlockSpec(memory_space=pl.ANY)] * 2,
        out_specs=tuple(whole(3)),
        scratch_shapes=[
            pltpu.VMEM((2, AGG), jnp.int32),
            pltpu.VMEM((AGG, B, PAIR), BF16),
            pltpu.SemaphoreType.DMA((5,)),
        ],
        compiler_params=pltpu.CompilerParams(vmem_limit_bytes=4 << 20),
        name="order",
    )(in_hbm(p_cols[0].T), in_hbm(p_vals))


def slot_table(cols, count_ref, wide_ref, table_ref):
    row = lax.broadcasted_iota(jnp.int32, (AGG, KA), 0)
    reach = ((cols & (PLANE - 1)) - lax.axis_index("col") * AGG + HALF) & (PLANE - 1)
    wide_ref[:AGG, :KA] = (cols // PLANE) * SPAN + reach - jnp.where(row < HALF, 0, HALF)
    places = wide_ref[...].T
    slot = lax.broadcasted_iota(jnp.int32, (KA, PAIR), 0)
    dest = lax.broadcasted_iota(jnp.int32, (KA, PAIR), 1)
    entry = slot // 2 + TILES * ((slot + dest) & 1) - EMPTY
    for q in range(AGG):
        place = jnp.broadcast_to(places[:KA, q : q + 1], (KA, PAIR))
        count = jnp.broadcast_to(count_ref[0:1, q : q + 1], (KA, PAIR))
        found = jnp.where((place == dest) & (slot < count), entry, 0)
        table_ref[q : q + 1, :] = EMPTY + jnp.sum(found, axis=0, keepdims=True)


def prepare_kernel(
    links_hbm, count_hbm, cols_hbm, a_hbm, r_hbm, links_ref, count_ref, slots_ref, restrict_ref,
    cols_ref, raw, sems, small_sems
):
    def fetch(q):
        return pltpu.make_async_copy(a_hbm.at[0, q], slots_ref.at[q, :, pl.ds(0, KA * B)], sems.at[q])

    small = [
        pltpu.make_async_copy(cols_hbm, cols_ref, small_sems.at[0]),
        pltpu.make_async_copy(r_hbm.at[0], raw, small_sems.at[1]),
        pltpu.make_async_copy(links_hbm.at[0], links_ref, small_sems.at[2]),
        pltpu.make_async_copy(count_hbm, count_ref, small_sems.at[3]),
    ]
    for copy in small:
        copy.start()
    for q in range(AGG):
        fetch(q).start()
    for copy in small:
        copy.wait()
    for q in range(0, AGG, 2):
        two = jnp.concatenate([ordered(raw[q], cols_ref, q), ordered(raw[q + 1], cols_ref, q + 1)], axis=0)
        at = (q % HALF) * B
        restrict_ref[q // HALF, :, at : at + PAIR] = two.T

    def row(q, carry):
        slots_ref[q, :, EMPTY * PAIR :] = jnp.zeros((B, PAIR), BF16)
        fetch(q).wait()
        for k in range(TILES):
            x = slots_ref[q, :, k * PAIR : (k + 1) * PAIR]
            slots_ref[q, :, (TILES + k) * PAIR : (TILES + k + 1) * PAIR] = swap_lanes(x)
        return carry

    lax.fori_loop(0, AGG, row, 0)


def prepare(a_cols, a_count, r_cols, a_vals, r_vals):
    return pl.pallas_call(
        prepare_kernel,
        out_shape=(
            jax.ShapeDtypeStruct((AGG, KA), jnp.int32),
            jax.ShapeDtypeStruct((1, AGG), jnp.int32),
            pltpu.VMEM((AGG, B, (EMPTY + 1) * PAIR), BF16),
            jax.ShapeDtypeStruct((2, PAIR, DEPTH), BF16),
        ),
        in_specs=[pl.BlockSpec(memory_space=pl.ANY)] * 5,
        out_specs=tuple(whole(4)),
        scratch_shapes=[
            pltpu.VMEM((2, AGG), jnp.int32),
            pltpu.VMEM((AGG, B, PAIR), BF16),
            pltpu.SemaphoreType.DMA((AGG,)),
            pltpu.SemaphoreType.DMA((4,)),
        ],
        compiler_params=pltpu.CompilerParams(vmem_limit_bytes=12 << 20),
        cost_estimate=pl.CostEstimate(flops=0, bytes_accessed=6 << 20, transcendentals=0),
        name="prepare",
    )(in_hbm(a_cols), in_hbm(a_count), in_hbm(r_cols[0].T), in_hbm(a_vals), in_hbm(r_vals))


def placed(x, shifted):
    if not shifted:
        return x
    lower = lax.broadcasted_iota(jnp.int32, (B, PAIR), 1) < B
    first, second = swap_lanes(x[:, :PAIR]), swap_lanes(x[:, PAIR:])
    return jnp.concatenate([jnp.where(lower, 0.0, first), jnp.where(lower, first, second)], axis=1)


def banded(blocks_ref, against, j):
    mid = DEPTH // 2

    def part(rows, depth):
        return jnp.dot(blocks_ref[rows, depth], against[depth], preferred_element_type=F32)

    everything, first, second = slice(0, DEPTH), slice(0, mid), slice(mid, DEPTH)
    if j == 1:
        return part(everything, everything)
    if j == 0:
        return jnp.concatenate([part(first, everything), part(second, second)], axis=0)
    return jnp.concatenate([part(first, first), part(second, everything)], axis=0)


def merged(low, high):
    lower = lax.broadcasted_iota(jnp.int32, (DEPTH, PAIR), 1) < B
    high = swap_lanes(high)
    return low + jnp.where(lower, 0.0, high), jnp.where(lower, high, 0.0)


def rows_of(ref, start):
    return ref[start : start + HALF].reshape(DEPTH, PAIR)


def gather(index_ref, slots_ref, s, half, j, into):
    lower = lax.broadcasted_iota(jnp.int32, (B, PAIR), 1) < B
    for e in range(HALF):
        q = half * HALF + e
        at = s * SPAN + j * HALF
        for tile in range(HALF // 2):
            rows, cols = slice(e * B, (e + 1) * B), slice(tile * PAIR, (tile + 1) * PAIR)
            if (j == 0 and tile < e // 2) or (j == 2 and tile > e // 2):
                early, near = e < HALF // 2, tile < HALF // 4
                if (j == 0 and (early or not near)) or (j == 2 and (near or not early)):
                    into[rows, cols] = jnp.zeros((B, PAIR), BF16)
                continue
            first = pl.multiple_of(index_ref[q, at + 2 * tile] * PAIR, PAIR)
            second = pl.multiple_of(index_ref[q, at + 2 * tile + 1] * PAIR, PAIR)
            into[rows, cols] = jnp.where(
                lower, slots_ref[q, :, pl.ds(first, PAIR)], slots_ref[q, :, pl.ds(second, PAIR)]
            )


def products_kernel(
    links_ref, count_ref, slots_ref, restrict_ref, left_ref, own_ref, right_ref, odd_ref, even_ref,
    edge_ref, sums_ref, own_out, before_out, after_out, index_ref, wide_ref, table_ref, band, sem
):
    slot_table(links_ref[...], count_ref, wide_ref, table_ref)
    to_scalars = pltpu.make_async_copy(table_ref, index_ref, sem)
    to_scalars.start()
    to_scalars.wait()

    turn = 0
    terms = []
    for n, near in ((2, own_ref), (0, odd_ref), (1, even_ref)):
        s = 1 if n == 2 else plane_of(1 - n)
        for half in range(2):
            sums = [None, None]
            for j in range(3):
                part = half + j
                if part in (0, 3) and n < 2:
                    gather(index_ref, slots_ref, s, half, j, edge_ref.at[2 * n + half])
                    continue
                if part in (0, 3):
                    against = rows_of(right_ref if part else left_ref, 0)
                else:
                    against = rows_of(near, (part - 1) * HALF)
                turn = (turn + 1) % 3
                gather(index_ref, slots_ref, s, half, j, band.at[turn])
                term = banded(band.at[turn], against, j)
                sums[part // 2] = term if sums[part // 2] is None else sums[part // 2] + term
            first, second = merged(*sums)
            if n < 2:
                sums_ref[n, half, :, :PAIR] = first
                sums_ref[n, half, :, PAIR:] = second
            else:
                fine = jnp.concatenate([first.astype(BF16), second.astype(BF16)], axis=1)
                terms.append(jnp.dot(restrict_ref[half], fine, preferred_element_type=F32))
    own_out[...] = terms[0][B:] + terms[1][:B]
    before_out[...] = placed(terms[0][:B], True).astype(BF16)
    after_out[...] = placed(terms[1][B:], True).astype(BF16)


def outer_kernel(
    edge_ref, sums_ref, restrict_ref, left_ref, right_ref, own_mid, before_mid, after_mid,
    own_ref, before_ref, after_ref
):
    lower = lax.broadcasted_iota(jnp.int32, (DEPTH, PAIR), 1) < B
    mid = slice(2 * PAIR, 4 * PAIR)
    own_ref[:, mid] = own_mid[...]
    before_ref[:, mid] = before_mid[...]
    after_ref[:, mid] = after_mid[...]
    for n in range(2):
        terms = []
        for half in range(2):
            first, second = sums_ref[n, half, :, :PAIR], sums_ref[n, half, :, PAIR:]
            against = rows_of(right_ref if half else left_ref, n * HALF)
            if half:
                against = swap_lanes(against)
            term = banded(edge_ref.at[2 * n + half], against, 2 * half)
            if half:
                first = first + jnp.where(lower, 0.0, term)
                second = second + jnp.where(lower, term, 0.0)
            else:
                first = first + term
            fine = jnp.concatenate([first.astype(BF16), second.astype(BF16)], axis=1)
            terms.append(jnp.dot(restrict_ref[half], fine, preferred_element_type=F32))
        cols = pl.ds(pl.multiple_of(plane_of(1 - n) * 2 * PAIR, PAIR), 2 * PAIR)
        own_ref[:, cols] = placed(terms[0][B:] + terms[1][:B], True)
        before_ref[:, cols] = terms[0][:B].astype(BF16)
        after_ref[:, cols] = terms[1][B:].astype(BF16)


OWN_AT = (0, 1, 3, 4, 5, 6)
ABOVE_AT = (1, 2, 3, 4, 6, 7)
BELOW_AT = (0, 1, 2, 3, 5, 6)


def join_kernel(own_ref, below_ref, above_ref, out_ref):
    for tile in range(8):
        width = PAIR if tile < 7 else B
        total = None
        for ref, places in ((own_ref, OWN_AT), (above_ref, ABOVE_AT), (below_ref, BELOW_AT)):
            if tile in places:
                at = places.index(tile) * PAIR
                piece = ref[:, at : at + width].astype(F32)
                total = piece if total is None else total + piece
        out_ref[0, :, tile * PAIR : tile * PAIR + width] = total


def in_hbm(x):
    return pltpu.with_memory_space_constraint(x, pltpu.HBM)


def whole(count):
    return [pl.BlockSpec(memory_space=pltpu.VMEM)] * count


def body(a_vals, a_cols, a_count, p_vals, p_cols, r_vals, r_cols):
    own, head, tail = order(p_vals, p_cols)
    odd = swap_rows(own, 1)
    even = swap_rows(own, 0)
    left = shift_cols(tail, 1)
    right = shift_cols(head, -1)
    links, count, slots, restrict = prepare(a_cols, a_count, r_cols, a_vals, r_vals)
    even, odd, left, right, slots = lax.optimization_barrier((even, odd, left, right, slots))
    both_left = shift_cols(jnp.concatenate([odd[HALF:], even[HALF:]], axis=0), 1)
    both_right = shift_cols(jnp.concatenate([odd[:HALF], even[:HALF]], axis=0), -1)

    edge, sums, own_mid, before_mid, after_mid = pl.pallas_call(
        products_kernel,
        out_shape=(
            jax.ShapeDtypeStruct((4, DEPTH, DEPTH), BF16),
            jax.ShapeDtypeStruct((2, 2, DEPTH, 2 * PAIR), F32),
            jax.ShapeDtypeStruct((B, 2 * PAIR), F32),
            jax.ShapeDtypeStruct((B, 2 * PAIR), BF16),
            jax.ShapeDtypeStruct((B, 2 * PAIR), BF16),
        ),
        in_specs=whole(9),
        out_specs=tuple(whole(5)),
        scratch_shapes=[
            pltpu.SMEM((AGG, PAIR), jnp.int32),
            pltpu.VMEM((PAIR, PAIR), jnp.int32),
            pltpu.VMEM((AGG, PAIR), jnp.int32),
            pltpu.VMEM((3, DEPTH, DEPTH), BF16),
            pltpu.SemaphoreType.DMA,
        ],
        compiler_params=pltpu.CompilerParams(vmem_limit_bytes=20 << 20),
        cost_estimate=pl.CostEstimate(flops=2 << 30, bytes_accessed=8 << 20, transcendentals=0),
        name="products",
    )(links, count, slots, restrict, left, own, right, odd, even)
    owned, before, after = pl.pallas_call(
        outer_kernel,
        out_shape=(
            jax.ShapeDtypeStruct((B, 6 * PAIR), F32),
            jax.ShapeDtypeStruct((B, 6 * PAIR), BF16),
            jax.ShapeDtypeStruct((B, 6 * PAIR), BF16),
        ),
        in_specs=whole(8),
        out_specs=tuple(whole(3)),
        compiler_params=pltpu.CompilerParams(vmem_limit_bytes=12 << 20),
        cost_estimate=pl.CostEstimate(flops=1 << 30, bytes_accessed=4 << 20, transcendentals=0),
        name="outer",
    )(edge, sums, restrict, both_left, both_right, own_mid, before_mid, after_mid)
    below = shift_cols(after, 1)
    above = shift_cols(before, -1)
    return pl.pallas_call(
        join_kernel,
        out_shape=jax.ShapeDtypeStruct((1, B, 15 * B), F32),
        in_specs=whole(3),
        out_specs=whole(1)[0],
        compiler_params=pltpu.CompilerParams(vmem_limit_bytes=4 << 20),
        name="join",
    )(owned, below, above)


def solution(mesh):
    return jax.shard_map(
        body,
        mesh=mesh,
        in_specs=(
            P("row", "col", None, None),
            P("row", "col", None),
            P("row", "col"),
            P("row", "col", None, None),
            P("row", "col", None),
            P("row", "col", None, None),
            P("row", "col", None),
        ),
        out_specs=P("row", "col", None),
        check_vma=False,
    )
```

time: 41.1 us -> 37.4 us (0.910)
  the two profiles are of different devices: /device:TPU:40 before, /device:TPU:50 now
where the time goes in v2:
time: 37.4 us; the launch traced here: 37.2 us
  starting transfers between devices  21.8 us (58%)
  Pallas kernels  12.9 us (34%)
  waiting for transfers between devices  2.31 us (6%)
    ppermute x6, starting transfers between devices, shift_cols(): lax.ppermute(value, 'col', [(i, (i + step) % count) for i in range(count)])  13.9 us
    ppermute x2, starting transfers between devices, swap_rows(): return lax.ppermute(value, 'row', pairs)  7.89 us
    pallas_call x1, Pallas kernels, body(): pl.pallas_call(products_kernel, out_shape=(jax.ShapeDtypeStruct((4, DEPTH...  4.89 us
    pallas_call x1, Pallas kernels, prepare(): pl.pallas_call(prepare_kernel, out_shape=(jax.ShapeDtypeStruct((AGG, KA),...  4.72 us
    ppermute x6, waiting for transfers between devices, shift_cols(): lax.ppermute(value, 'col', [(i, (i + step) % count) for i in range(count)])  2.31 us
    pallas_call x1, Pallas kernels, order(): pl.pallas_call(order_kernel, out_shape=(jax.ShapeDtypeStruct((AGG, B, PAI...  1.39 us
    pallas_call x1, Pallas kernels, body(): pl.pallas_call(outer_kernel, out_shape=(jax.ShapeDtypeStruct((B, 6 * PAIR...  1.2 us
  transfers between devices with their start and end apart: 8, of which 1 were waited for; matrix products, arithmetic and copies ran while one was open for 0% of the time, Pallas kernels for 26%

profile of v2, /device:TPU:50, one launch (start us, length us, event | category | flops | bytes accessed | tf_op | source)
XLA Modules:
  0.0 37.2 jit_solution(3423006423254930923)
XLA Ops:
  0.0 1.4 %order.1 = (bf16[16,64,128]{2,1,0:T(8,128)(2,1)S(1)}, bf16[8,64,128]{2,1,0:T(8,128)(2,1)S(1)}, bf16[8,64,128]{2,1,0:T(8,128)(2,1)S(1)}) custom-call(s32[2,16]{1,0:T(2,128)} %bitcast.6, bf16[1,16,64,128]{3,2,1,0:T(8,128)(2,1)} %p_hbm.1), custom_call_target="tpu_custom_call" | custom-call | tf_op jit(solution)/shard_map/order/pallas_call | solution.py:79
  1.4 3.4 %collective-permute-start.1 = (bf16[16,64,128]{2,1,0:T(8,128)(2,1)S(1)}, bf16[16,64,128]{2,1,0:T(8,128)(2,1)S(1)}, u32[]{:S(2)}, u32[]{:S(2)}) collective-permute-start(bf16[16,64,128]{2,1,0:T(8,128)(2,1)S(1)} %get-tuple-element.27.own_ref), channel_id=1, source_target_pairs={{16,32},{32,16},{48,64},{64,48},{80,96},{96,80},{112,128},{128,112... | collective-permute-start | bytes 786440 | tf_op jit(solution)/shard_map/ppermute | solution.py:32
  4.8 4.5 %collective-permute-start = (bf16[16,64,128]{2,1,0:T(8,128)(2,1)S(1)}, bf16[16,64,128]{2,1,0:T(8,128)(2,1)S(1)}, u32[]{:S(2)}, u32[]{:S(2)}) collective-permute-start(bf16[16,64,128]{2,1,0:T(8,128)(2,1)S(1)} %get-tuple-element.27.own_ref), channel_id=1, source_target_pairs={{0,16},{16,0},{32,48},{48,32},{64,80},{80,64},{96,112},{112,96},{1... | collective-permute-start | bytes 786440 | tf_op jit(solution)/shard_map/ppermute | solution.py:32
  9.3 0.0 collective-permute-start.2
  9.3 7.9 %collective-permute-start.3 = (bf16[8,64,128]{2,1,0:T(8,128)(2,1)S(1)}, bf16[8,64,128]{2,1,0:T(8,128)(2,1)S(1)}, u32[]{:S(2)}, u32[]{:S(2)}) collective-permute-start(bf16[8,64,128]{2,1,0:T(8,128)(2,1)S(1)} %get-tuple-element.29), channel_id=1, source_target_pairs={{0,15},{1,0},{2,1},{3,2},{4,3},{5,4},{6,5},{7,6},{8,7},{9,8},{10,9... | collective-permute-start | bytes 393224 | tf_op jit(solution)/shard_map/ppermute | solution.py:25
  17.3 4.7 %prepare.1 = (s32[16,32]{1,0:T(8,128)S(1)}, s32[1,16]{1,0:T(1,128)S(1)}, bf16[16,64,4224]{2,1,0:T(8,128)(2,1)S(1)}, bf16[2,128,512]{2,1,0:T(8,128)(2,1)S(1)}) custom-call(s32[1,16,32]{2,1,0:T(8,128)} %links_hbm.1, s32[1,16]{1,0:T(1,128)} %count_hbm.1, s32[2,16]{1,0:T(2,128)} %bitcast.7, bf16[1,16,64,2048]{3,2,1,0:T(8,128)(2,1)} %a_hbm.1, ...), custom_call_target="tpu_custom_call" | custom-call | bytes 6291456 | tf_op jit(solution)/shard_map/prepare/pallas_call | solution.py:145
  22.0 0.0 collective-permute-done.2.left_ref
  22.0 0.0 collective-permute-done.3.right_ref
  22.0 0.0 collective-permute-done.1.odd_ref
  22.0 0.0 collective-permute-done.even_ref
  22.1 0.0 collective-permute-start.4
  22.2 2.9 %collective-permute-start.5 = (bf16[16,64,128]{2,1,0:T(8,128)(2,1)S(1)}, bf16[16,64,128]{2,1,0:T(8,128)(2,1)S(1)}, u32[]{:S(2)}, u32[]{:S(2)}) collective-permute-start(bf16[16,64,128]{2,1,0:T(8,128)(2,1)S(1)} %pad_maximum_fusion.1), channel_id=1, source_target_pairs={{0,15},{1,0},{2,1},{3,2},{4,3},{5,4},{6,5},{7,6},{8,7},{9,8},{10,9... | collective-permute-start | bytes 786440 | tf_op jit(solution)/shard_map/ppermute | solution.py:25
  25.1 4.9 %products.1 = (bf16[4,512,512]{2,1,0:T(8,128)(2,1)S(1)}, f32[2,2,512,256]{3,2,1,0:T(8,128)S(1)}, f32[64,256]{1,0:T(8,128)S(1)}, bf16[64,256]{1,0:T(8,128)(2,1)S(1)}, bf16[64,256]{1,0:T(8,128)(2,1)S(1)}) custom-call(s32[16,32]{1,0:T(8,128)S(1)} %get-tuple-element.25.links_ref, s32[1,16]{1,0:T(1,128)S(1)} %get-tuple-element.26.count_ref, ...), custom_call_target="tpu_custom_call" | custom-call | flops 2147483648 | bytes 8388608 | tf_op jit(solution)/shard_map/products/pallas_call | solution.py:324
  30.0 0.0 collective-permute-done.4.left_ref
  30.0 0.0 collective-permute-done.5.right_ref
  30.0 1.2 %outer.1 = (f32[64,768]{1,0:T(8,128)S(1)}, bf16[64,768]{1,0:T(8,128)(2,1)S(1)}, bf16[64,768]{1,0:T(8,128)(2,1)S(1)}) custom-call(bf16[4,512,512]{2,1,0:T(8,128)(2,1)S(1)} %get-tuple-element.37.edge_ref, f32[2,2,512,256]{3,2,1,0:T(8,128)S(1)} %get-tuple-element.38.sums_ref, bf16[2,128,512]{2,1,0:T(8,128)(2,1)S(1)} %get-tuple-element.32.restrict_ref, ...), custom_call_target="tpu_custom_call" | custom-call | flops 1073741824 | bytes 4194304 | tf_op jit(solution)/shard_map/outer/pallas_call | solution.py:346
  31.2 0.0 collective-permute-start.6
  31.3 2.9 %collective-permute-start.7 = (bf16[64,768]{1,0:T(8,128)(2,1)S(1)}, bf16[64,768]{1,0:T(8,128)(2,1)S(1)}, u32[]{:S(2)}, u32[]{:S(2)}) collective-permute-start(bf16[64,768]{1,0:T(8,128)(2,1)S(1)} %get-tuple-element.44), channel_id=1, source_target_pairs={{0,15},{1,0},{2,1},{3,2},{4,3},{5,4},{6,5},{7,6},{8,7},{9,8},{10,9... | collective-permute-start | bytes 294920 | tf_op jit(solution)/shard_map/ppermute | solution.py:25
  34.2 2.3 %collective-permute-done.6.below_ref = bf16[64,768]{1,0:T(8,128)(2,1)S(1)} collective-permute-done((bf16[64,768]{1,0:T(8,128)(2,1)S(1)}, bf16[64,768]{1,0:T(8,128)(2,1)S(1)}, u32[]{:S(2)}, u32[]{:S(2)}) %collective-permute-start.6) | collective-permute-done | bytes 98336 | tf_op jit(solution)/shard_map/ppermute | solution.py:25
  36.5 0.0 collective-permute-done.7.above_ref
  36.5 0.7 %join.1 = f32[1,64,960]{2,1,0:T(8,128)} custom-call(f32[64,768]{1,0:T(8,128)S(1)} %get-tuple-element.42.own_ref, bf16[64,768]{1,0:T(8,128)(2,1)S(1)} %collective-permute-done.6.below_ref, bf16[64,768]{1,0:T(8,128)(2,1)S(1)} %collective-permute-done.7.above_ref), custom_call_target="tpu_custom_call" | custom-call | tf_op jit(solution)/shard_map/join/pallas_call | solution.py:361
  (3 shorter events, 0.1 us)
Async XLA Ops:
  1.4 20.6 %collective-permute-start.1 = (bf16[16,64,128]{2,1,0:T(8,128)(2,1)S(1)}, bf16[16,64,128]{2,1,0:T(8,128)(2,1)S(1)}, u32[]{:S(2)}, u32[]{:S(2)}) collective-permute-start(bf16[16,64,128]{2,1,0:T(8,128)(2,1)S(1)} %get-tuple-element.27.own_ref), channel_id=1, source_target_pairs={{16,32},{32,16},{48,64},{64,48},{80,96},{96,80},{112,128},{128,112... | collective-permute-start | bytes 786440 | tf_op jit(solution)/shard_map/ppermute | solution.py:32
  4.8 17.2 %collective-permute-start = (bf16[16,64,128]{2,1,0:T(8,128)(2,1)S(1)}, bf16[16,64,128]{2,1,0:T(8,128)(2,1)S(1)}, u32[]{:S(2)}, u32[]{:S(2)}) collective-permute-start(bf16[16,64,128]{2,1,0:T(8,128)(2,1)S(1)} %get-tuple-element.27.own_ref), channel_id=1, source_target_pairs={{0,16},{16,0},{32,48},{48,32},{64,80},{80,64},{96,112},{112,96},{1... | collective-permute-start | bytes 786440 | tf_op jit(solution)/shard_map/ppermute | solution.py:32
  9.3 12.7 %collective-permute-start.2 = (bf16[8,64,128]{2,1,0:T(8,128)(2,1)S(1)}, bf16[8,64,128]{2,1,0:T(8,128)(2,1)S(1)}, u32[]{:S(2)}, u32[]{:S(2)}) collective-permute-start(bf16[8,64,128]{2,1,0:T(8,128)(2,1)S(1)} %get-tuple-element.28), channel_id=1, source_target_pairs={{0,1},{1,2},{2,3},{3,4},{4,5},{5,6},{6,7},{7,8},{8,9},{9,10},{10,1... | collective-permute-start | bytes 393224 | tf_op jit(solution)/shard_map/ppermute | solution.py:25
  9.3 12.7 %collective-permute-start.3 = (bf16[8,64,128]{2,1,0:T(8,128)(2,1)S(1)}, bf16[8,64,128]{2,1,0:T(8,128)(2,1)S(1)}, u32[]{:S(2)}, u32[]{:S(2)}) collective-permute-start(bf16[8,64,128]{2,1,0:T(8,128)(2,1)S(1)} %get-tuple-element.29), channel_id=1, source_target_pairs={{0,15},{1,0},{2,1},{3,2},{4,3},{5,4},{6,5},{7,6},{8,7},{9,8},{10,9... | collective-permute-start | bytes 393224 | tf_op jit(solution)/shard_map/ppermute | solution.py:25
  22.1 7.9 %collective-permute-start.4 = (bf16[16,64,128]{2,1,0:T(8,128)(2,1)S(1)}, bf16[16,64,128]{2,1,0:T(8,128)(2,1)S(1)}, u32[]{:S(2)}, u32[]{:S(2)}) collective-permute-start(bf16[16,64,128]{2,1,0:T(8,128)(2,1)S(1)} %pad_maximum_fusion), channel_id=1, source_target_pairs={{0,1},{1,2},{2,3},{3,4},{4,5},{5,6},{6,7},{7,8},{8,9},{9,10},{10,1... | collective-permute-start | bytes 786440 | tf_op jit(solution)/shard_map/ppermute | solution.py:25
  22.2 7.9 %collective-permute-start.5 = (bf16[16,64,128]{2,1,0:T(8,128)(2,1)S(1)}, bf16[16,64,128]{2,1,0:T(8,128)(2,1)S(1)}, u32[]{:S(2)}, u32[]{:S(2)}) collective-permute-start(bf16[16,64,128]{2,1,0:T(8,128)(2,1)S(1)} %pad_maximum_fusion.1), channel_id=1, source_target_pairs={{0,15},{1,0},{2,1},{3,2},{4,3},{5,4},{6,5},{7,6},{8,7},{9,8},{10,9... | collective-permute-start | bytes 786440 | tf_op jit(solution)/shard_map/ppermute | solution.py:25
  31.2 5.3 %collective-permute-start.6 = (bf16[64,768]{1,0:T(8,128)(2,1)S(1)}, bf16[64,768]{1,0:T(8,128)(2,1)S(1)}, u32[]{:S(2)}, u32[]{:S(2)}) collective-permute-start(bf16[64,768]{1,0:T(8,128)(2,1)S(1)} %get-tuple-element.43), channel_id=1, source_target_pairs={{0,1},{1,2},{2,3},{3,4},{4,5},{5,6},{6,7},{7,8},{8,9},{9,10},{10,1... | collective-permute-start | bytes 294920 | tf_op jit(solution)/shard_map/ppermute | solution.py:25
  31.3 5.2 %collective-permute-start.7 = (bf16[64,768]{1,0:T(8,128)(2,1)S(1)}, bf16[64,768]{1,0:T(8,128)(2,1)S(1)}, u32[]{:S(2)}, u32[]{:S(2)}) collective-permute-start(bf16[64,768]{1,0:T(8,128)(2,1)S(1)} %get-tuple-element.44), channel_id=1, source_target_pairs={{0,15},{1,0},{2,1},{3,2},{4,3},{5,4},{6,5},{7,6},{8,7},{9,8},{10,9... | collective-permute-start | bytes 294920 | tf_op jit(solution)/shard_map/ppermute | solution.py:25

commit v3 on v2

--- a/solution.py
+++ b/solution.py
@@ -51,7 +51,7 @@
 
 
 def order_kernel(cols_hbm, p_hbm, all_ref, head_ref, tail_ref, cols_ref, raw, sems):
-    parts = 4
+    parts = 2
     size = AGG // parts
     cols_copy = pltpu.make_async_copy(cols_hbm, cols_ref, sems.at[parts])
     cols_copy.start()
@@ -84,7 +84,7 @@
         scratch_shapes=[
             pltpu.VMEM((2, AGG), jnp.int32),
             pltpu.VMEM((AGG, B, PAIR), BF16),
-            pltpu.SemaphoreType.DMA((5,)),
+            pltpu.SemaphoreType.DMA((3,)),
         ],
         compiler_params=pltpu.CompilerParams(vmem_limit_bytes=4 << 20),
         name="order",
@@ -107,8 +107,8 @@
 
 
 def prepare_kernel(
-    links_hbm, count_hbm, cols_hbm, a_hbm, r_hbm, links_ref, count_ref, slots_ref, restrict_ref,
-    cols_ref, raw, sems, small_sems
+    links_hbm, count_hbm, cols_hbm, a_hbm, r_hbm, index_ref, slots_ref, restrict_ref,
+    links_ref, count_ref, cols_ref, wide_ref, table_ref, raw, sems, small_sems
 ):
     def fetch(q):
         return pltpu.make_async_copy(a_hbm.at[0, q], slots_ref.at[q, :, pl.ds(0, KA * B)], sems.at[q])
@@ -119,17 +119,10 @@
         pltpu.make_async_copy(links_hbm.at[0], links_ref, small_sems.at[2]),
         pltpu.make_async_copy(count_hbm, count_ref, small_sems.at[3]),
     ]
-    for copy in small:
-        copy.start()
     for q in range(AGG):
         fetch(q).start()
     for copy in small:
-        copy.wait()
-    for q in range(0, AGG, 2):
-        two = jnp.concatenate([ordered(raw[q], cols_ref, q), ordered(raw[q + 1], cols_ref, q + 1)], axis=0)
-        at = (q % HALF) * B
-        restrict_ref[q // HALF, :, at : at + PAIR] = two.T
-
+        copy.start(priority=1)
     def row(q, carry):
         slots_ref[q, :, EMPTY * PAIR :] = jnp.zeros((B, PAIR), BF16)
         fetch(q).wait()
@@ -139,24 +132,42 @@
         return carry
 
     lax.fori_loop(0, AGG, row, 0)
+    for copy in small:
+        copy.wait()
+    slot_table(links_ref[...], count_ref, wide_ref, table_ref)
+    to_scalars = pltpu.make_async_copy(table_ref, index_ref, small_sems.at[4])
+    to_scalars.start()
+    unit = jnp.where(
+        lax.broadcasted_iota(jnp.int32, (PAIR, PAIR), 0) == lax.broadcasted_iota(jnp.int32, (PAIR, PAIR), 1), 1.0, 0.0
+    ).astype(BF16)
+    for q in range(0, AGG, 2):
+        two = jnp.concatenate([ordered(raw[q], cols_ref, q), ordered(raw[q + 1], cols_ref, q + 1)], axis=0)
+        at = (q % HALF) * B
+        turned = lax.dot_general(unit, two, (((1,), (1,)), ((), ())), preferred_element_type=F32)
+        restrict_ref[q // HALF, :, at : at + PAIR] = turned.astype(BF16)
+
+    to_scalars.wait()
 
 
 def prepare(a_cols, a_count, r_cols, a_vals, r_vals):
     return pl.pallas_call(
         prepare_kernel,
         out_shape=(
-            jax.ShapeDtypeStruct((AGG, KA), jnp.int32),
-            jax.ShapeDtypeStruct((1, AGG), jnp.int32),
+            pltpu.SMEM((AGG, PAIR), jnp.int32),
             pltpu.VMEM((AGG, B, (EMPTY + 1) * PAIR), BF16),
             jax.ShapeDtypeStruct((2, PAIR, DEPTH), BF16),
         ),
         in_specs=[pl.BlockSpec(memory_space=pl.ANY)] * 5,
-        out_specs=tuple(whole(4)),
+        out_specs=(pl.BlockSpec(memory_space=pltpu.SMEM), *whole(2)),
         scratch_shapes=[
+            pltpu.VMEM((AGG, KA), jnp.int32),
+            pltpu.VMEM((1, AGG), jnp.int32),
             pltpu.VMEM((2, AGG), jnp.int32),
+            pltpu.VMEM((PAIR, PAIR), jnp.int32),
+            pltpu.VMEM((AGG, PAIR), jnp.int32),
             pltpu.VMEM((AGG, B, PAIR), BF16),
             pltpu.SemaphoreType.DMA((AGG,)),
-            pltpu.SemaphoreType.DMA((4,)),
+            pltpu.SemaphoreType.DMA((5,)),
         ],
         compiler_params=pltpu.CompilerParams(vmem_limit_bytes=12 << 20),
         cost_estimate=pl.CostEstimate(flops=0, bytes_accessed=6 << 20, transcendentals=0),
@@ -216,14 +227,9 @@
 
 
 def products_kernel(
-    links_ref, count_ref, slots_ref, restrict_ref, left_ref, own_ref, right_ref, odd_ref, even_ref,
-    edge_ref, sums_ref, own_out, before_out, after_out, index_ref, wide_ref, table_ref, band, sem
+    index_ref, slots_ref, restrict_ref, left_ref, own_ref, right_ref, odd_ref, even_ref,
+    edge_ref, sums_ref, own_out, before_out, after_out, band
 ):
-    slot_table(links_ref[...], count_ref, wide_ref, table_ref)
-    to_scalars = pltpu.make_async_copy(table_ref, index_ref, sem)
-    to_scalars.start()
-    to_scalars.wait()
-
     turn = 0
     terms = []
     for n, near in ((2, own_ref), (0, odd_ref), (1, even_ref)):
@@ -316,7 +322,7 @@
     even = swap_rows(own, 0)
     left = shift_cols(tail, 1)
     right = shift_cols(head, -1)
-    links, count, slots, restrict = prepare(a_cols, a_count, r_cols, a_vals, r_vals)
+    index, slots, restrict = prepare(a_cols, a_count, r_cols, a_vals, r_vals)
     even, odd, left, right, slots = lax.optimization_barrier((even, odd, left, right, slots))
     both_left = shift_cols(jnp.concatenate([odd[HALF:], even[HALF:]], axis=0), 1)
     both_right = shift_cols(jnp.concatenate([odd[:HALF], even[:HALF]], axis=0), -1)
@@ -330,19 +336,13 @@
             jax.ShapeDtypeStruct((B, 2 * PAIR), BF16),
             jax.ShapeDtypeStruct((B, 2 * PAIR), BF16),
         ),
-        in_specs=whole(9),
+        in_specs=[pl.BlockSpec(memory_space=pltpu.SMEM)] + whole(7),
         out_specs=tuple(whole(5)),
-        scratch_shapes=[
-            pltpu.SMEM((AGG, PAIR), jnp.int32),
-            pltpu.VMEM((PAIR, PAIR), jnp.int32),
-            pltpu.VMEM((AGG, PAIR), jnp.int32),
-            pltpu.VMEM((3, DEPTH, DEPTH), BF16),
-            pltpu.SemaphoreType.DMA,
-        ],
+        scratch_shapes=[pltpu.VMEM((3, DEPTH, DEPTH), BF16)],
         compiler_params=pltpu.CompilerParams(vmem_limit_bytes=20 << 20),
         cost_estimate=pl.CostEstimate(flops=2 << 30, bytes_accessed=8 << 20, transcendentals=0),
         name="products",
-    )(links, count, slots, restrict, left, own, right, odd, even)
+    )(index, slots, restrict, left, own, right, odd, even)
     owned, before, after = pl.pallas_call(
         outer_kernel,
         out_shape=(

time: 37.4 us -> 36 us (0.963)
  the two profiles are of different devices: /device:TPU:50 before, /device:TPU:58 now
where the time goes in v3:
time: 36 us; the launch traced here: 35.9 us
  starting transfers between devices  21.8 us (61%)
  Pallas kernels  11.2 us (31%)
  waiting for transfers between devices  2.6 us (7%)
    ppermute x6, starting transfers between devices, shift_cols(): lax.ppermute(value, 'col', [(i, (i + step) % count) for i in range(count)])  13.9 us
    ppermute x2, starting transfers between devices, swap_rows(): return lax.ppermute(value, 'row', pairs)  7.89 us
    pallas_call x1, Pallas kernels, prepare(): pl.pallas_call(prepare_kernel, out_shape=(pltpu.SMEM((AGG, PAIR), jnp.int...  4.38 us
    pallas_call x1, Pallas kernels, body(): pl.pallas_call(products_kernel, out_shape=(jax.ShapeDtypeStruct((4, DEPTH...  3.69 us
    ppermute x6, waiting for transfers between devices, shift_cols(): lax.ppermute(value, 'col', [(i, (i + step) % count) for i in range(count)])  2.6 us
    pallas_call x1, Pallas kernels, order(): pl.pallas_call(order_kernel, out_shape=(jax.ShapeDtypeStruct((AGG, B, PAI...  1.22 us
    pallas_call x1, Pallas kernels, body(): pl.pallas_call(outer_kernel, out_shape=(jax.ShapeDtypeStruct((B, 6 * PAIR...  1.19 us
    pallas_call x1, Pallas kernels, body(): pl.pallas_call(join_kernel, out_shape=jax.ShapeDtypeStruct((1, B, 15 * B)...  0.73 us
  transfers between devices with their start and end apart: 8, of which 2 were waited for; matrix products, arithmetic and copies ran while one was open for 0% of the time, Pallas kernels for 23%

profile of v3, /device:TPU:58, one launch (start us, length us, event | category | flops | bytes accessed | tf_op | source)
XLA Modules:
  0.0 35.9 jit_solution(17462672687538352780)
XLA Ops:
  0.0 1.2 %order.1 = (bf16[16,64,128]{2,1,0:T(8,128)(2,1)S(1)}, bf16[8,64,128]{2,1,0:T(8,128)(2,1)S(1)}, bf16[8,64,128]{2,1,0:T(8,128)(2,1)S(1)}) custom-call(s32[2,16]{1,0:T(2,128)} %bitcast.6, bf16[1,16,64,128]{3,2,1,0:T(8,128)(2,1)} %p_hbm.1), custom_call_target="tpu_custom_call" | custom-call | tf_op jit(solution)/shard_map/order/pallas_call | solution.py:79
  1.2 3.4 %collective-permute-start.1 = (bf16[16,64,128]{2,1,0:T(8,128)(2,1)S(1)}, bf16[16,64,128]{2,1,0:T(8,128)(2,1)S(1)}, u32[]{:S(2)}, u32[]{:S(2)}) collective-permute-start(bf16[16,64,128]{2,1,0:T(8,128)(2,1)S(1)} %get-tuple-element.25.own_ref), channel_id=1, source_target_pairs={{16,32},{32,16},{48,64},{64,48},{80,96},{96,80},{112,128},{128,112... | collective-permute-start | bytes 786440 | tf_op jit(solution)/shard_map/ppermute | solution.py:32
  4.6 4.5 %collective-permute-start = (bf16[16,64,128]{2,1,0:T(8,128)(2,1)S(1)}, bf16[16,64,128]{2,1,0:T(8,128)(2,1)S(1)}, u32[]{:S(2)}, u32[]{:S(2)}) collective-permute-start(bf16[16,64,128]{2,1,0:T(8,128)(2,1)S(1)} %get-tuple-element.25.own_ref), channel_id=1, source_target_pairs={{0,16},{16,0},{32,48},{48,32},{64,80},{80,64},{96,112},{112,96},{1... | collective-permute-start | bytes 786440 | tf_op jit(solution)/shard_map/ppermute | solution.py:32
  9.1 0.0 collective-permute-start.2
  9.2 7.9 %collective-permute-start.3 = (bf16[8,64,128]{2,1,0:T(8,128)(2,1)S(1)}, bf16[8,64,128]{2,1,0:T(8,128)(2,1)S(1)}, u32[]{:S(2)}, u32[]{:S(2)}) collective-permute-start(bf16[8,64,128]{2,1,0:T(8,128)(2,1)S(1)} %get-tuple-element.27), channel_id=1, source_target_pairs={{0,15},{1,0},{2,1},{3,2},{4,3},{5,4},{6,5},{7,6},{8,7},{9,8},{10,9... | collective-permute-start | bytes 393224 | tf_op jit(solution)/shard_map/ppermute | solution.py:25
  17.1 4.4 %prepare.1 = (s32[16,128]{1,0:T(8,128)S(4)}, bf16[16,64,4224]{2,1,0:T(8,128)(2,1)S(1)}, bf16[2,128,512]{2,1,0:T(8,128)(2,1)S(1)}) custom-call(s32[1,16,32]{2,1,0:T(8,128)} %links_hbm.1, s32[1,16]{1,0:T(1,128)} %count_hbm.1, s32[2,16]{1,0:T(2,128)} %bitcast.7, bf16[1,16,64,2048]{3,2,1,0:T(8,128)(2,1)} %a_hbm.1, bf16[1,16,64,128]{3,2,1,0:T(8,128)(2,1)} %r_hbm.1), custom_call_target="tpu_custom_call" | custom-call | bytes 6291456 | tf_op jit(solution)/shard_map/prepare/pallas_call | solution.py:153
  21.5 0.0 collective-permute-done.2.left_ref
  21.5 0.0 collective-permute-done.3.right_ref
  21.5 0.0 collective-permute-done.1.odd_ref
  21.5 0.0 collective-permute-done.even_ref
  21.6 0.0 collective-permute-start.4
  21.7 2.9 %collective-permute-start.5 = (bf16[16,64,128]{2,1,0:T(8,128)(2,1)S(1)}, bf16[16,64,128]{2,1,0:T(8,128)(2,1)S(1)}, u32[]{:S(2)}, u32[]{:S(2)}) collective-permute-start(bf16[16,64,128]{2,1,0:T(8,128)(2,1)S(1)} %pad_maximum_fusion.1), channel_id=1, source_target_pairs={{0,15},{1,0},{2,1},{3,2},{4,3},{5,4},{6,5},{7,6},{8,7},{9,8},{10,9... | collective-permute-start | bytes 786440 | tf_op jit(solution)/shard_map/ppermute | solution.py:25
  24.6 3.7 %products.1 = (bf16[4,512,512]{2,1,0:T(8,128)(2,1)S(1)}, f32[2,2,512,256]{3,2,1,0:T(8,128)S(1)}, f32[64,256]{1,0:T(8,128)S(1)}, bf16[64,256]{1,0:T(8,128)(2,1)S(1)}, bf16[64,256]{1,0:T(8,128)(2,1)S(1)}) custom-call(s32[16,128]{1,0:T(8,128)S(4)} %get-tuple-element.24.index_ref, bf16[16,64,4224]{2,1,0:T(8,128)(2,1)S(1)} %get-tuple-element.29.slots_ref, ...), custom_call_target="tpu_custom_call" | custom-call | flops 2147483648 | bytes 8388608 | tf_op jit(solution)/shard_map/products/pallas_call | solution.py:330
  28.3 0.3 collective-permute-done.4.left_ref
  28.6 0.0 collective-permute-done.5.right_ref
  28.6 1.2 %outer.1 = (f32[64,768]{1,0:T(8,128)S(1)}, bf16[64,768]{1,0:T(8,128)(2,1)S(1)}, bf16[64,768]{1,0:T(8,128)(2,1)S(1)}) custom-call(bf16[4,512,512]{2,1,0:T(8,128)(2,1)S(1)} %get-tuple-element.35.edge_ref, f32[2,2,512,256]{3,2,1,0:T(8,128)S(1)} %get-tuple-element.36.sums_ref, bf16[2,128,512]{2,1,0:T(8,128)(2,1)S(1)} %get-tuple-element.30.restrict_ref, ...), custom_call_target="tpu_custom_call" | custom-call | flops 1073741824 | bytes 4194304 | tf_op jit(solution)/shard_map/outer/pallas_call | solution.py:346
  29.8 0.0 collective-permute-start.6
  29.9 3.0 %collective-permute-start.7 = (bf16[64,768]{1,0:T(8,128)(2,1)S(1)}, bf16[64,768]{1,0:T(8,128)(2,1)S(1)}, u32[]{:S(2)}, u32[]{:S(2)}) collective-permute-start(bf16[64,768]{1,0:T(8,128)(2,1)S(1)} %get-tuple-element.42), channel_id=1, source_target_pairs={{0,15},{1,0},{2,1},{3,2},{4,3},{5,4},{6,5},{7,6},{8,7},{9,8},{10,9... | collective-permute-start | bytes 294920 | tf_op jit(solution)/shard_map/ppermute | solution.py:25
  32.9 2.3 %collective-permute-done.6.below_ref = bf16[64,768]{1,0:T(8,128)(2,1)S(1)} collective-permute-done((bf16[64,768]{1,0:T(8,128)(2,1)S(1)}, bf16[64,768]{1,0:T(8,128)(2,1)S(1)}, u32[]{:S(2)}, u32[]{:S(2)}) %collective-permute-start.6) | collective-permute-done | bytes 98336 | tf_op jit(solution)/shard_map/ppermute | solution.py:25
  35.1 0.0 collective-permute-done.7.above_ref
  35.2 0.7 %join.1 = f32[1,64,960]{2,1,0:T(8,128)} custom-call(f32[64,768]{1,0:T(8,128)S(1)} %get-tuple-element.40.own_ref, bf16[64,768]{1,0:T(8,128)(2,1)S(1)} %collective-permute-done.6.below_ref, bf16[64,768]{1,0:T(8,128)(2,1)S(1)} %collective-permute-done.7.above_ref), custom_call_target="tpu_custom_call" | custom-call | tf_op jit(solution)/shard_map/join/pallas_call | solution.py:361
  (3 shorter events, 0.1 us)
Async XLA Ops:
  1.2 20.3 %collective-permute-start.1 = (bf16[16,64,128]{2,1,0:T(8,128)(2,1)S(1)}, bf16[16,64,128]{2,1,0:T(8,128)(2,1)S(1)}, u32[]{:S(2)}, u32[]{:S(2)}) collective-permute-start(bf16[16,64,128]{2,1,0:T(8,128)(2,1)S(1)} %get-tuple-element.25.own_ref), channel_id=1, source_target_pairs={{16,32},{32,16},{48,64},{64,48},{80,96},{96,80},{112,128},{128,112... | collective-permute-start | bytes 786440 | tf_op jit(solution)/shard_map/ppermute | solution.py:32
  4.6 16.9 %collective-permute-start = (bf16[16,64,128]{2,1,0:T(8,128)(2,1)S(1)}, bf16[16,64,128]{2,1,0:T(8,128)(2,1)S(1)}, u32[]{:S(2)}, u32[]{:S(2)}) collective-permute-start(bf16[16,64,128]{2,1,0:T(8,128)(2,1)S(1)} %get-tuple-element.25.own_ref), channel_id=1, source_target_pairs={{0,16},{16,0},{32,48},{48,32},{64,80},{80,64},{96,112},{112,96},{1... | collective-permute-start | bytes 786440 | tf_op jit(solution)/shard_map/ppermute | solution.py:32
  9.1 12.4 %collective-permute-start.2 = (bf16[8,64,128]{2,1,0:T(8,128)(2,1)S(1)}, bf16[8,64,128]{2,1,0:T(8,128)(2,1)S(1)}, u32[]{:S(2)}, u32[]{:S(2)}) collective-permute-start(bf16[8,64,128]{2,1,0:T(8,128)(2,1)S(1)} %get-tuple-element.26), channel_id=1, source_target_pairs={{0,1},{1,2},{2,3},{3,4},{4,5},{5,6},{6,7},{7,8},{8,9},{9,10},{10,1... | collective-permute-start | bytes 393224 | tf_op jit(solution)/shard_map/ppermute | solution.py:25
  9.2 12.3 %collective-permute-start.3 = (bf16[8,64,128]{2,1,0:T(8,128)(2,1)S(1)}, bf16[8,64,128]{2,1,0:T(8,128)(2,1)S(1)}, u32[]{:S(2)}, u32[]{:S(2)}) collective-permute-start(bf16[8,64,128]{2,1,0:T(8,128)(2,1)S(1)} %get-tuple-element.27), channel_id=1, source_target_pairs={{0,15},{1,0},{2,1},{3,2},{4,3},{5,4},{6,5},{7,6},{8,7},{9,8},{10,9... | collective-permute-start | bytes 393224 | tf_op jit(solution)/shard_map/ppermute | solution.py:25
  21.6 7.0 %collective-permute-start.4 = (bf16[16,64,128]{2,1,0:T(8,128)(2,1)S(1)}, bf16[16,64,128]{2,1,0:T(8,128)(2,1)S(1)}, u32[]{:S(2)}, u32[]{:S(2)}) collective-permute-start(bf16[16,64,128]{2,1,0:T(8,128)(2,1)S(1)} %pad_maximum_fusion), channel_id=1, source_target_pairs={{0,1},{1,2},{2,3},{3,4},{4,5},{5,6},{6,7},{7,8},{8,9},{9,10},{10,1... | collective-permute-start | bytes 786440 | tf_op jit(solution)/shard_map/ppermute | solution.py:25
  21.7 7.0 %collective-permute-start.5 = (bf16[16,64,128]{2,1,0:T(8,128)(2,1)S(1)}, bf16[16,64,128]{2,1,0:T(8,128)(2,1)S(1)}, u32[]{:S(2)}, u32[]{:S(2)}) collective-permute-start(bf16[16,64,128]{2,1,0:T(8,128)(2,1)S(1)} %pad_maximum_fusion.1), channel_id=1, source_target_pairs={{0,15},{1,0},{2,1},{3,2},{4,3},{5,4},{6,5},{7,6},{8,7},{9,8},{10,9... | collective-permute-start | bytes 786440 | tf_op jit(solution)/shard_map/ppermute | solution.py:25
  29.8 5.3 %collective-permute-start.6 = (bf16[64,768]{1,0:T(8,128)(2,1)S(1)}, bf16[64,768]{1,0:T(8,128)(2,1)S(1)}, u32[]{:S(2)}, u32[]{:S(2)}) collective-permute-start(bf16[64,768]{1,0:T(8,128)(2,1)S(1)} %get-tuple-element.41), channel_id=1, source_target_pairs={{0,1},{1,2},{2,3},{3,4},{4,5},{5,6},{6,7},{7,8},{8,9},{9,10},{10,1... | collective-permute-start | bytes 294920 | tf_op jit(solution)/shard_map/ppermute | solution.py:25
  29.9 5.3 %collective-permute-start.7 = (bf16[64,768]{1,0:T(8,128)(2,1)S(1)}, bf16[64,768]{1,0:T(8,128)(2,1)S(1)}, u32[]{:S(2)}, u32[]{:S(2)}) collective-permute-start(bf16[64,768]{1,0:T(8,128)(2,1)S(1)} %get-tuple-element.42), channel_id=1, source_target_pairs={{0,15},{1,0},{2,1},{3,2},{4,3},{5,4},{6,5},{7,6},{8,7},{9,8},{10,9... | collective-permute-start | bytes 294920 | tf_op jit(solution)/shard_map/ppermute | solution.py:25

commit v4 on v3

--- a/solution.py
+++ b/solution.py
@@ -123,6 +123,7 @@
         fetch(q).start()
     for copy in small:
         copy.start(priority=1)
+
     def row(q, carry):
         slots_ref[q, :, EMPTY * PAIR :] = jnp.zeros((B, PAIR), BF16)
         fetch(q).wait()
@@ -131,7 +132,7 @@
             slots_ref[q, :, (TILES + k) * PAIR : (TILES + k + 1) * PAIR] = swap_lanes(x)
         return carry
 
-    lax.fori_loop(0, AGG, row, 0)
+    lax.fori_loop(0, 12, row, 0)
     for copy in small:
         copy.wait()
     slot_table(links_ref[...], count_ref, wide_ref, table_ref)
@@ -145,7 +146,7 @@
         at = (q % HALF) * B
         turned = lax.dot_general(unit, two, (((1,), (1,)), ((), ())), preferred_element_type=F32)
         restrict_ref[q // HALF, :, at : at + PAIR] = turned.astype(BF16)
-
+    lax.fori_loop(12, AGG, row, 0)
     to_scalars.wait()
 
 

time: 36 us -> 35.5 us (0.986)
  Pallas kernels: 11.2 us -> 10.7 us
    pallas_call x1, Pallas kernels: 4.38 us -> 3.83 us  [prepare(): pl.pallas_call(prepare_kernel, out_shape=(pltpu.SMEM((AGG, PAIR), jnp.int...]
  transfers between devices with their start and end apart: 8 -> 8, of which waited for: 2 -> 2; matrix products, arithmetic and copies ran while one was open for 0% -> 0% of each run, Pallas kernels for 23% -> 21%
where the time goes in v4:
time: 35.5 us; the launch traced here: 35.3 us
  starting transfers between devices  21.8 us (61%)
  Pallas kernels  10.7 us (30%)
  waiting for transfers between devices  2.61 us (7%)
    ppermute x6, starting transfers between devices, shift_cols(): lax.ppermute(value, 'col', [(i, (i + step) % count) for i in range(count)])  13.9 us
    ppermute x2, starting transfers between devices, swap_rows(): return lax.ppermute(value, 'row', pairs)  7.89 us
    pallas_call x1, Pallas kernels, prepare(): pl.pallas_call(prepare_kernel, out_shape=(pltpu.SMEM((AGG, PAIR), jnp.int...  3.83 us
    pallas_call x1, Pallas kernels, body(): pl.pallas_call(products_kernel, out_shape=(jax.ShapeDtypeStruct((4, DEPTH...  3.68 us
    ppermute x6, waiting for transfers between devices, shift_cols(): lax.ppermute(value, 'col', [(i, (i + step) % count) for i in range(count)])  2.61 us
    pallas_call x1, Pallas kernels, order(): pl.pallas_call(order_kernel, out_shape=(jax.ShapeDtypeStruct((AGG, B, PAI...  1.22 us
    pallas_call x1, Pallas kernels, body(): pl.pallas_call(outer_kernel, out_shape=(jax.ShapeDtypeStruct((B, 6 * PAIR...  1.19 us
    pallas_call x1, Pallas kernels, body(): pl.pallas_call(join_kernel, out_shape=jax.ShapeDtypeStruct((1, B, 15 * B)...  0.73 us
  transfers between devices with their start and end apart: 8, of which 2 were waited for; matrix products, arithmetic and copies ran while one was open for 0% of the time, Pallas kernels for 21%

profile of v4, /device:TPU:58, one launch (start us, length us, event | category | flops | bytes accessed | tf_op | source)
XLA Modules:
  0.0 35.3 jit_solution(9316295637003912765)
XLA Ops:
  0.0 1.2 %order.1 = (bf16[16,64,128]{2,1,0:T(8,128)(2,1)S(1)}, bf16[8,64,128]{2,1,0:T(8,128)(2,1)S(1)}, bf16[8,64,128]{2,1,0:T(8,128)(2,1)S(1)}) custom-call(s32[2,16]{1,0:T(2,128)} %bitcast.6, bf16[1,16,64,128]{3,2,1,0:T(8,128)(2,1)} %p_hbm.1), custom_call_target="tpu_custom_call" | custom-call | tf_op jit(solution)/shard_map/order/pallas_call | solution.py:79
  1.2 3.4 %collective-permute-start.1 = (bf16[16,64,128]{2,1,0:T(8,128)(2,1)S(1)}, bf16[16,64,128]{2,1,0:T(8,128)(2,1)S(1)}, u32[]{:S(2)}, u32[]{:S(2)}) collective-permute-start(bf16[16,64,128]{2,1,0:T(8,128)(2,1)S(1)} %get-tuple-element.25.own_ref), channel_id=1, source_target_pairs={{16,32},{32,16},{48,64},{64,48},{80,96},{96,80},{112,128},{128,112... | collective-permute-start | bytes 786440 | tf_op jit(solution)/shard_map/ppermute | solution.py:32
  4.6 4.5 %collective-permute-start = (bf16[16,64,128]{2,1,0:T(8,128)(2,1)S(1)}, bf16[16,64,128]{2,1,0:T(8,128)(2,1)S(1)}, u32[]{:S(2)}, u32[]{:S(2)}) collective-permute-start(bf16[16,64,128]{2,1,0:T(8,128)(2,1)S(1)} %get-tuple-element.25.own_ref), channel_id=1, source_target_pairs={{0,16},{16,0},{32,48},{48,32},{64,80},{80,64},{96,112},{112,96},{1... | collective-permute-start | bytes 786440 | tf_op jit(solution)/shard_map/ppermute | solution.py:32
  9.1 0.0 collective-permute-start.2
  9.2 7.9 %collective-permute-start.3 = (bf16[8,64,128]{2,1,0:T(8,128)(2,1)S(1)}, bf16[8,64,128]{2,1,0:T(8,128)(2,1)S(1)}, u32[]{:S(2)}, u32[]{:S(2)}) collective-permute-start(bf16[8,64,128]{2,1,0:T(8,128)(2,1)S(1)} %get-tuple-element.27), channel_id=1, source_target_pairs={{0,15},{1,0},{2,1},{3,2},{4,3},{5,4},{6,5},{7,6},{8,7},{9,8},{10,9... | collective-permute-start | bytes 393224 | tf_op jit(solution)/shard_map/ppermute | solution.py:25
  17.1 3.8 %prepare.1 = (s32[16,128]{1,0:T(8,128)S(4)}, bf16[16,64,4224]{2,1,0:T(8,128)(2,1)S(1)}, bf16[2,128,512]{2,1,0:T(8,128)(2,1)S(1)}) custom-call(s32[1,16,32]{2,1,0:T(8,128)} %links_hbm.1, s32[1,16]{1,0:T(1,128)} %count_hbm.1, s32[2,16]{1,0:T(2,128)} %bitcast.7, bf16[1,16,64,2048]{3,2,1,0:T(8,128)(2,1)} %a_hbm.1, bf16[1,16,64,128]{3,2,1,0:T(8,128)(2,1)} %r_hbm.1), custom_call_target="tpu_custom_call" | custom-call | bytes 6291456 | tf_op jit(solution)/shard_map/prepare/pallas_call | solution.py:154
  20.9 0.0 collective-permute-done.2.left_ref
  20.9 0.0 collective-permute-done.3.right_ref
  21.0 0.0 collective-permute-done.1.odd_ref
  21.0 0.0 collective-permute-done.even_ref
  21.1 0.0 collective-permute-start.4
  21.1 2.9 %collective-permute-start.5 = (bf16[16,64,128]{2,1,0:T(8,128)(2,1)S(1)}, bf16[16,64,128]{2,1,0:T(8,128)(2,1)S(1)}, u32[]{:S(2)}, u32[]{:S(2)}) collective-permute-start(bf16[16,64,128]{2,1,0:T(8,128)(2,1)S(1)} %pad_maximum_fusion.1), channel_id=1, source_target_pairs={{0,15},{1,0},{2,1},{3,2},{4,3},{5,4},{6,5},{7,6},{8,7},{9,8},{10,9... | collective-permute-start | bytes 786440 | tf_op jit(solution)/shard_map/ppermute | solution.py:25
  24.1 3.7 %products.1 = (bf16[4,512,512]{2,1,0:T(8,128)(2,1)S(1)}, f32[2,2,512,256]{3,2,1,0:T(8,128)S(1)}, f32[64,256]{1,0:T(8,128)S(1)}, bf16[64,256]{1,0:T(8,128)(2,1)S(1)}, bf16[64,256]{1,0:T(8,128)(2,1)S(1)}) custom-call(s32[16,128]{1,0:T(8,128)S(4)} %get-tuple-element.24.index_ref, bf16[16,64,4224]{2,1,0:T(8,128)(2,1)S(1)} %get-tuple-element.29.slots_ref, ...), custom_call_target="tpu_custom_call" | custom-call | flops 2147483648 | bytes 8388608 | tf_op jit(solution)/shard_map/products/pallas_call | solution.py:331
  27.8 0.3 collective-permute-done.4.left_ref
  28.1 0.0 collective-permute-done.5.right_ref
  28.1 1.2 %outer.1 = (f32[64,768]{1,0:T(8,128)S(1)}, bf16[64,768]{1,0:T(8,128)(2,1)S(1)}, bf16[64,768]{1,0:T(8,128)(2,1)S(1)}) custom-call(bf16[4,512,512]{2,1,0:T(8,128)(2,1)S(1)} %get-tuple-element.35.edge_ref, f32[2,2,512,256]{3,2,1,0:T(8,128)S(1)} %get-tuple-element.36.sums_ref, bf16[2,128,512]{2,1,0:T(8,128)(2,1)S(1)} %get-tuple-element.30.restrict_ref, ...), custom_call_target="tpu_custom_call" | custom-call | flops 1073741824 | bytes 4194304 | tf_op jit(solution)/shard_map/outer/pallas_call | solution.py:347
  29.3 0.0 collective-permute-start.6
  29.3 3.0 %collective-permute-start.7 = (bf16[64,768]{1,0:T(8,128)(2,1)S(1)}, bf16[64,768]{1,0:T(8,128)(2,1)S(1)}, u32[]{:S(2)}, u32[]{:S(2)}) collective-permute-start(bf16[64,768]{1,0:T(8,128)(2,1)S(1)} %get-tuple-element.42), channel_id=1, source_target_pairs={{0,15},{1,0},{2,1},{3,2},{4,3},{5,4},{6,5},{7,6},{8,7},{9,8},{10,9... | collective-permute-start | bytes 294920 | tf_op jit(solution)/shard_map/ppermute | solution.py:25
  32.3 2.3 %collective-permute-done.6.below_ref = bf16[64,768]{1,0:T(8,128)(2,1)S(1)} collective-permute-done((bf16[64,768]{1,0:T(8,128)(2,1)S(1)}, bf16[64,768]{1,0:T(8,128)(2,1)S(1)}, u32[]{:S(2)}, u32[]{:S(2)}) %collective-permute-start.6) | collective-permute-done | bytes 98336 | tf_op jit(solution)/shard_map/ppermute | solution.py:25
  34.6 0.0 collective-permute-done.7.above_ref
  34.6 0.7 %join.1 = f32[1,64,960]{2,1,0:T(8,128)} custom-call(f32[64,768]{1,0:T(8,128)S(1)} %get-tuple-element.40.own_ref, bf16[64,768]{1,0:T(8,128)(2,1)S(1)} %collective-permute-done.6.below_ref, bf16[64,768]{1,0:T(8,128)(2,1)S(1)} %collective-permute-done.7.above_ref), custom_call_target="tpu_custom_call" | custom-call | tf_op jit(solution)/shard_map/join/pallas_call | solution.py:362
  (3 shorter events, 0.1 us)
Async XLA Ops:
  1.2 19.7 %collective-permute-start.1 = (bf16[16,64,128]{2,1,0:T(8,128)(2,1)S(1)}, bf16[16,64,128]{2,1,0:T(8,128)(2,1)S(1)}, u32[]{:S(2)}, u32[]{:S(2)}) collective-permute-start(bf16[16,64,128]{2,1,0:T(8,128)(2,1)S(1)} %get-tuple-element.25.own_ref), channel_id=1, source_target_pairs={{16,32},{32,16},{48,64},{64,48},{80,96},{96,80},{112,128},{128,112... | collective-permute-start | bytes 786440 | tf_op jit(solution)/shard_map/ppermute | solution.py:32
  4.6 16.3 %collective-permute-start = (bf16[16,64,128]{2,1,0:T(8,128)(2,1)S(1)}, bf16[16,64,128]{2,1,0:T(8,128)(2,1)S(1)}, u32[]{:S(2)}, u32[]{:S(2)}) collective-permute-start(bf16[16,64,128]{2,1,0:T(8,128)(2,1)S(1)} %get-tuple-element.25.own_ref), channel_id=1, source_target_pairs={{0,16},{16,0},{32,48},{48,32},{64,80},{80,64},{96,112},{112,96},{1... | collective-permute-start | bytes 786440 | tf_op jit(solution)/shard_map/ppermute | solution.py:32
  9.1 11.8 %collective-permute-start.2 = (bf16[8,64,128]{2,1,0:T(8,128)(2,1)S(1)}, bf16[8,64,128]{2,1,0:T(8,128)(2,1)S(1)}, u32[]{:S(2)}, u32[]{:S(2)}) collective-permute-start(bf16[8,64,128]{2,1,0:T(8,128)(2,1)S(1)} %get-tuple-element.26), channel_id=1, source_target_pairs={{0,1},{1,2},{2,3},{3,4},{4,5},{5,6},{6,7},{7,8},{8,9},{9,10},{10,1... | collective-permute-start | bytes 393224 | tf_op jit(solution)/shard_map/ppermute | solution.py:25
  9.2 11.8 %collective-permute-start.3 = (bf16[8,64,128]{2,1,0:T(8,128)(2,1)S(1)}, bf16[8,64,128]{2,1,0:T(8,128)(2,1)S(1)}, u32[]{:S(2)}, u32[]{:S(2)}) collective-permute-start(bf16[8,64,128]{2,1,0:T(8,128)(2,1)S(1)} %get-tuple-element.27), channel_id=1, source_target_pairs={{0,15},{1,0},{2,1},{3,2},{4,3},{5,4},{6,5},{7,6},{8,7},{9,8},{10,9... | collective-permute-start | bytes 393224 | tf_op jit(solution)/shard_map/ppermute | solution.py:25
  21.1 7.0 %collective-permute-start.4 = (bf16[16,64,128]{2,1,0:T(8,128)(2,1)S(1)}, bf16[16,64,128]{2,1,0:T(8,128)(2,1)S(1)}, u32[]{:S(2)}, u32[]{:S(2)}) collective-permute-start(bf16[16,64,128]{2,1,0:T(8,128)(2,1)S(1)} %pad_maximum_fusion), channel_id=1, source_target_pairs={{0,1},{1,2},{2,3},{3,4},{4,5},{5,6},{6,7},{7,8},{8,9},{9,10},{10,1... | collective-permute-start | bytes 786440 | tf_op jit(solution)/shard_map/ppermute | solution.py:25
  21.1 7.0 %collective-permute-start.5 = (bf16[16,64,128]{2,1,0:T(8,128)(2,1)S(1)}, bf16[16,64,128]{2,1,0:T(8,128)(2,1)S(1)}, u32[]{:S(2)}, u32[]{:S(2)}) collective-permute-start(bf16[16,64,128]{2,1,0:T(8,128)(2,1)S(1)} %pad_maximum_fusion.1), channel_id=1, source_target_pairs={{0,15},{1,0},{2,1},{3,2},{4,3},{5,4},{6,5},{7,6},{8,7},{9,8},{10,9... | collective-permute-start | bytes 786440 | tf_op jit(solution)/shard_map/ppermute | solution.py:25
  29.3 5.3 %collective-permute-start.6 = (bf16[64,768]{1,0:T(8,128)(2,1)S(1)}, bf16[64,768]{1,0:T(8,128)(2,1)S(1)}, u32[]{:S(2)}, u32[]{:S(2)}) collective-permute-start(bf16[64,768]{1,0:T(8,128)(2,1)S(1)} %get-tuple-element.41), channel_id=1, source_target_pairs={{0,1},{1,2},{2,3},{3,4},{4,5},{5,6},{6,7},{7,8},{8,9},{9,10},{10,1... | collective-permute-start | bytes 294920 | tf_op jit(solution)/shard_map/ppermute | solution.py:25
  29.3 5.3 %collective-permute-start.7 = (bf16[64,768]{1,0:T(8,128)(2,1)S(1)}, bf16[64,768]{1,0:T(8,128)(2,1)S(1)}, u32[]{:S(2)}, u32[]{:S(2)}) collective-permute-start(bf16[64,768]{1,0:T(8,128)(2,1)S(1)} %get-tuple-element.42), channel_id=1, source_target_pairs={{0,15},{1,0},{2,1},{3,2},{4,3},{5,4},{6,5},{7,6},{8,7},{9,8},{10,9... | collective-permute-start | bytes 294920 | tf_op jit(solution)/shard_map/ppermute | solution.py:25
